TPU v7x, 256 devices: a whole 4x4x8 slice. The times are simulated.
256 devices in a mesh: lon: 32 (over z, y_hi, core), lat: 8 (over y_lo, x).
Axes of the slice: x: 4, y: 4 (y_hi: 2, y_lo: 2; y = y_hi * 2 + y_lo), z: 8, core: 2. Of those that a mesh axis runs over, the one named last changes fastest.
Arguments:
- zonal_flow: float32 [4, 1024, 4096], P(None, 'lat', 'lon'), as said below
- meridional_flow: float32 [4, 1024, 4096], P(None, 'lat', 'lon'), as said below
- tracers: float32 [3, 4, 1024, 4096], P(None, None, 'lat', 'lon'), may hold values from -6 to 6
- sea_mask: int32 [4, 1024, 4096], P(None, 'lat', 'lon'), may hold values from 0 to 1, as said below
- diffusivity: float32 [3, 1024, 4096], P(None, 'lat', 'lon'), may hold values from 0.05 to 5
Outputs:
- zonal_out: float32 [4, 1024, 4096], P(None, 'lat', 'lon')
- meridional_out: float32 [4, 1024, 4096], P(None, 'lat', 'lon')
- tracers_out: float32 [3, 4, 1024, 4096], P(None, None, 'lat', 'lon')
Inputs may be any that keep to these rules, and one draw needn't show every extreme that they name: There is a stream function s of shape [4, 1024, 4096] on cell corners with |s| <= 0.12, zero below row 0 and periodic in longitude, such that zonal_flow[k, j, i] = s[k, j - 1, i] - s[k, j, i]; the discrete divergence of the two velocities vanishes. meridional_flow[k, j, i] = s[k, j, i] - s[k, j, i - 1] with the same stream function s as zonal_flow. `sea_mask`: A cell is sea only where the cell above it, at level k - 1, is sea.
All inputs are finite; a program needn't handle non-finite values.
Results may differ from a plain program's by a relative error of at most 0.0003.
Values sent between devices are 32-bit elements; how exact they have to be, the bound alone decides.
A program may use at most 64 MiB of HBM per device.

v0:
```python
import functools
import math

import jax
import jax.numpy as jnp
from jax import lax
from jax.experimental import pallas as pl
from jax.experimental.pallas import tpu as pltpu
from jax.sharding import PartitionSpec as P

K = 4
T = 3
NSUB = 3
B = 128
H = 8
E = B + 2 * H
R = E // 8
F32 = jnp.float32
MESH = pl.DeviceIdType.MESH
coriolis_peak = 0.5


def exchange(nlat, nlon, u, v, q, m, rn, rs, mn, ms, pe, pw, xv, mv, ke, kw, load, send, recv):
    lat = lax.axis_index("lat")
    lon = lax.axis_index("lon")
    top = lat == nlat - 1
    bottom = lat == 0
    east = lax.rem(lon + 1, nlon)
    west = lax.rem(lon + nlon - 1, nlon)
    n_lat = jnp.where(top, lat, lat + 1)
    n_mid = jnp.where(top, nlon - 1 - lon, lon)
    n_west = jnp.where(top, lax.rem(nlon - lon, nlon), west)
    n_east = jnp.where(top, lax.rem(2 * nlon - 2 - lon, nlon), east)
    s_lat = jnp.maximum(lat - 1, 0)
    own_w = n_west == lon
    own_e = n_east == lon

    def at(row, column):
        return {"lat": row, "lon": column}

    loads = [
        pltpu.make_async_copy(u, xv.at[0:K], load.at[0]),
        pltpu.make_async_copy(v, xv.at[K : 2 * K], load.at[1]),
        pltpu.make_async_copy(q, xv.at[2 * K :], load.at[2]),
        pltpu.make_async_copy(m, mv, load.at[3]),
    ]
    for copy in loads:
        copy.start()

    barrier = pltpu.get_barrier_semaphore()

    def greet(row, column):
        pl.semaphore_signal(barrier, inc=1, device_id=at(row, column), device_id_type=MESH)

    greet(lat, east)
    greet(lat, west)
    greet(n_lat, n_mid)

    @pl.when(jnp.logical_not(top & own_w))
    def _():
        greet(n_lat, n_west)

    @pl.when(jnp.logical_not(top & own_e))
    def _():
        greet(n_lat, n_east)

    @pl.when(jnp.logical_not(bottom))
    def _():
        greet(s_lat, lon)
        greet(s_lat, west)
        greet(s_lat, east)

    peers = (
        3
        + jnp.where(top & own_w, 0, 1)
        + jnp.where(top & own_e, 0, 1)
        + jnp.where(bottom, 0, 3)
    )
    pl.semaphore_wait(barrier, peers)

    def remote(src, dst, slot, row, column):
        return pltpu.make_async_remote_copy(
            src_ref=src,
            dst_ref=dst,
            send_sem=send.at[slot],
            recv_sem=recv.at[slot],
            device_id=at(row, column),
            device_id_type=MESH,
        )

    hi = pl.ds(B - H, H)
    lo = pl.ds(0, H)

    def rows(part, fields, marks, base, row, column):
        return [
            remote(u.at[:, part], fields.at[0:K], base, row, column),
            remote(v.at[:, part], fields.at[K : 2 * K], base + 1, row, column),
            remote(q.at[:, part], fields.at[2 * K :], base + 2, row, column),
            remote(m.at[:, part], marks, base + 3, row, column),
        ]

    to_north = rows(hi, rs, ms, 8, n_lat, n_mid)
    over_fold = rows(hi, rn, mn, 2, n_lat, n_mid)
    to_south = rows(lo, rn, mn, 2, s_lat, lon)

    @pl.when(top)
    def _():
        for copy in over_fold:
            copy.start()

    @pl.when(jnp.logical_not(top))
    def _():
        for copy in to_north:
            copy.start()

    @pl.when(jnp.logical_not(bottom))
    def _():
        for copy in to_south:
            copy.start()

    for copy in loads:
        copy.wait()

    group = lax.broadcasted_iota(jnp.int32, (8, B), 1) // 8

    def pack(i, carry):
        part = pl.ds(pl.multiple_of(i * 8, 8), 8)
        for half in range(2):
            packed_w = jnp.zeros((8, B), F32)
            packed_e = jnp.zeros((8, B), F32)
            for k in range(K):
                for f in range(4 if half == 0 else 2):
                    if half == 1:
                        x = xv[f * K + k, part]
                    elif f < T:
                        x = xv[2 * K + f * K + k, part]
                    else:
                        x = mv[k, part].astype(F32)
                    j = 4 * k + f
                    x = pltpu.roll(x, 8 * j, 1) if j else x
                    packed_w = jnp.where(group == j, x, packed_w)
                    packed_e = jnp.where(group == (j - 1) % 16, x, packed_e)
            kw[half, part] = packed_w
            ke[half, part] = packed_e
        return carry

    lax.fori_loop(0, B // 8, pack, 0)

    middle = pl.ds(H, B)
    beyond = pl.ds(H + B, H)
    sends = [
        remote(ke, pw.at[:, middle], 1, lat, east),
        remote(kw, pe.at[:, middle], 0, lat, west),
    ]
    for copy in sends:
        copy.start()
    north_east = remote(ke.at[:, hi], pw.at[:, lo], 13, n_lat, n_east)
    north_west = remote(kw.at[:, hi], pe.at[:, lo], 12, n_lat, n_west)
    fold_west = remote(kw.at[:, hi], pw.at[:, beyond], 7, n_lat, n_west)
    fold_east = remote(ke.at[:, hi], pe.at[:, beyond], 6, n_lat, n_east)
    self_west = pltpu.make_async_copy(kw.at[:, hi], pw.at[:, beyond], load.at[4])
    self_east = pltpu.make_async_copy(ke.at[:, hi], pe.at[:, beyond], load.at[5])
    south_east = remote(ke.at[:, lo], pw.at[:, beyond], 7, s_lat, east)
    south_west = remote(kw.at[:, lo], pe.at[:, beyond], 6, s_lat, west)

    @pl.when(jnp.logical_not(top))
    def _():
        north_east.start()
        north_west.start()

    @pl.when(top & own_w)
    def _():
        self_west.start()

    @pl.when(top & jnp.logical_not(own_w))
    def _():
        fold_west.start()

    @pl.when(top & own_e)
    def _():
        self_east.start()

    @pl.when(top & jnp.logical_not(own_e))
    def _():
        fold_east.start()

    @pl.when(jnp.logical_not(bottom))
    def _():
        south_east.start()
        south_west.start()

    for copy in sends:
        copy.wait_send()

    @pl.when(top)
    def _():
        for copy in over_fold:
            copy.wait_send()

    @pl.when(jnp.logical_not(top))
    def _():
        for copy in to_north:
            copy.wait_send()
        north_east.wait_send()
        north_west.wait_send()

    @pl.when(top & own_w)
    def _():
        self_west.wait()

    @pl.when(top & jnp.logical_not(own_w))
    def _():
        fold_west.wait_send()

    @pl.when(top & own_e)
    def _():
        self_east.wait()

    @pl.when(top & jnp.logical_not(own_e))
    def _():
        fold_east.wait_send()

    @pl.when(jnp.logical_not(bottom))
    def _():
        for copy in to_south:
            copy.wait_send()
        south_east.wait_send()
        south_west.wait_send()

    for copy in sends:
        copy.wait_recv()
    for copy in to_south:
        copy.wait_recv()

    @pl.when(jnp.logical_not(top & own_w))
    def _():
        south_east.wait_recv()

    @pl.when(jnp.logical_not(top & own_e))
    def _():
        south_west.wait_recv()

    @pl.when(jnp.logical_not(bottom))
    def _():
        for copy in to_north:
            copy.wait_recv()
        north_east.wait_recv()
        north_west.wait_recv()


def exchanged(nlat, nlon, u, v, q, m):
    any_space = pl.BlockSpec(memory_space=pl.ANY)
    return pl.pallas_call(
        functools.partial(exchange, nlat, nlon),
        out_shape=(
            jax.ShapeDtypeStruct(((2 + T) * K, H, B), F32),
            jax.ShapeDtypeStruct(((2 + T) * K, H, B), F32),
            jax.ShapeDtypeStruct((K, H, B), jnp.int32),
            jax.ShapeDtypeStruct((K, H, B), jnp.int32),
            jax.ShapeDtypeStruct((2, E, B), F32),
            jax.ShapeDtypeStruct((2, E, B), F32),
        ),
        in_specs=[any_space] * 4,
        out_specs=[any_space] * 6,
        scratch_shapes=[
            pltpu.VMEM(((2 + T) * K, B, B), F32),
            pltpu.VMEM((K, B, B), jnp.int32),
            pltpu.VMEM((2, B, B), F32),
            pltpu.VMEM((2, B, B), F32),
            pltpu.SemaphoreType.DMA((6,)),
            pltpu.SemaphoreType.DMA((14,)),
            pltpu.SemaphoreType.DMA((14,)),
        ],
        compiler_params=pltpu.CompilerParams(
            collective_id=0, has_side_effects=True, vmem_limit_bytes=32 * 2**20
        ),
    )(u, v, q, m)


def minmod(a, b):
    return jnp.maximum(jnp.minimum(a, b), jnp.minimum(jnp.maximum(a, b), 0.0))


def following(x):
    return pltpu.roll(x, B - 1, 1)


def preceding(x):
    return pltpu.roll(x, 1, 1)


def above(x):
    return pltpu.roll(x, 7, 0)


def below(x):
    return pltpu.roll(x, 1, 0)


def rolled(x, amount):
    return pltpu.roll(x, amount % B, 1) if amount % B else x


def flipped(x, index):
    x = jnp.take_along_axis(x, index, axis=1)
    backward = 7 - lax.broadcasted_iota(jnp.int32, (8, B), 0)
    return jnp.take_along_axis(x, backward, axis=0)


def solve(x, coupling):
    carried = []
    inverse = []
    for k in range(K):
        divisor = 1.0
        if k < K - 1:
            divisor = divisor + coupling[k]
        if k > 0:
            divisor = divisor + coupling[k - 1] * (1.0 - carried[k - 1])
        inverse.append(1.0 / divisor)
        if k < K - 1:
            carried.append(coupling[k] * inverse[k])
    results = []
    for field in x:
        scaled = [field[0] * inverse[0]]
        for k in range(1, K):
            scaled.append((field[k] + coupling[k - 1] * scaled[k - 1]) * inverse[k])
        solved = [scaled[K - 1]]
        for k in range(K - 2, -1, -1):
            solved.insert(0, scaled[k] + carried[k] * solved[0])
        results.append(solved)
    return results


def compute(
    nlat, u, v, q, m, d, rn, rs, mn, ms, pe, pw, uo, vo, qo,
    ext, mext, dext, pks, flow, new, tr, wet, cx, cy, fold, load, store,
):
    lat = lax.axis_index("lat")
    top = lat == nlat - 1
    bottom = lat == 0
    middle = pl.ds(H, B)
    lo = pl.ds(0, H)
    beyond = pl.ds(H + B, H)
    N = (2 + T) * K
    copies = [
        pltpu.make_async_copy(u, ext.at[0:K, middle], load.at[0]),
        pltpu.make_async_copy(v, ext.at[K : 2 * K, middle], load.at[1]),
        pltpu.make_async_copy(q, ext.at[2 * K :, middle], load.at[2]),
        pltpu.make_async_copy(m, mext.at[:, middle], load.at[3]),
        pltpu.make_async_copy(rn, ext.at[:, beyond], load.at[4]),
        pltpu.make_async_copy(rs, ext.at[:, lo], load.at[5]),
        pltpu.make_async_copy(mn, mext.at[:, beyond], load.at[6]),
        pltpu.make_async_copy(ms, mext.at[:, lo], load.at[7]),
        pltpu.make_async_copy(pe, pks.at[0], load.at[8]),
        pltpu.make_async_copy(pw, pks.at[1], load.at[9]),
        pltpu.make_async_copy(d, dext.at[:, middle], load.at[10]),
    ]
    for copy in copies:
        copy.start()
    for copy in copies[:-1]:
        copy.wait()

    lane = lax.broadcasted_iota(jnp.int32, (8, B), 1)
    sub = lax.broadcasted_iota(jnp.int32, (8, B), 0)

    @pl.when(bottom)
    def _():
        ext[:, lo] = jnp.zeros((N, H, B), F32)
        mext[:, lo] = jnp.zeros((K, H, B), jnp.int32)
        pks[:, :, lo] = jnp.zeros((2, 2, H, B), F32)

    @pl.when(top)
    def _():
        whole = B - 1 - lane
        for f in range(N):
            x = flipped(ext[f, beyond], whole)
            ext[f, beyond] = -x if f < 2 * K else x
        for k in range(K):
            mext[k, beyond] = flipped(mext[k, beyond].astype(F32), whole).astype(jnp.int32)
        within = 7 - lane % 8
        from_east = (lane // 8 + 15) % 16 * 8 + within
        from_west = (lane // 8 + 1) % 16 * 8 + within
        for half in range(2):
            x = flipped(pks[0, half, beyond], from_east)
            pks[0, half, beyond] = -x if half else x
            x = flipped(pks[1, half, beyond], from_west)
            pks[1, half, beyond] = -x if half else x

    place = lane % 32
    level = lane // 32
    own_hi = place < 10
    own_lo = place >= 22
    far_hi = (place >= 10) & (place < 16)
    far_lo = (place >= 16) & (place < 22)
    is_hi = [own_hi & (level == k) for k in range(K)]
    is_lo = [own_lo & (level == k) for k in range(K)]

    for r in range(R):
        strided = pl.ds(r, 8, stride=R)
        packs = [[pks[side, half, strided] for half in range(2)] for side in range(2)]
        for f in range(2 + T + 1):
            edge = jnp.zeros((8, B), F32)
            for k in range(K):
                if f < 2 + T:
                    x = ext[f * K + k, strided]
                else:
                    x = mext[k, strided].astype(F32)
                if f < 2:
                    flow[f, k, r] = x
                elif f < 2 + T:
                    tr[f - 2, k, r] = x
                else:
                    wet[k, r] = x
                edge = jnp.where(is_hi[k], rolled(x, 32 * k + 10), edge)
                edge = jnp.where(is_lo[k], rolled(x, 32 * k + 22), edge)
            half, slot = (1, f) if f < 2 else (0, f - 2)
            edge = jnp.where(far_hi, rolled(packs[0][half], 10 - 8 * slot), edge)
            edge = jnp.where(far_lo, rolled(packs[1][half], 22 - 8 * slot), edge)
            if f < 2:
                flow[f, K, r] = edge
            elif f < 2 + T:
                tr[f - 2, K, r] = edge
            else:
                wet[K, r] = edge

    def coriolis(offset):
        row = lat * B + R * sub + lane - H
        ny = nlat * B
        return coriolis_peak * jnp.sin(math.pi * ((row.astype(F32) + offset) / ny - 0.5))

    cor_u = coriolis(0.5)
    cor_v = coriolis(1.0)
    last = top & (sub == 7)

    def prepare(i, carry):
        def get(f, r):
            if r == -1:
                return below(flow[f, i, R - 1])
            if r == R:
                return above(flow[f, i, 0])
            return flow[f, i, r]

        us, vs = get(0, -1), get(1, -1)
        u0, v0 = get(0, 0), get(1, 0)
        w0 = wet[i, 0]
        for r in range(R):
            un, vn = get(0, r + 1), get(1, r + 1)
            wn = wet[i, r + 1] if r < R - 1 else above(wet[i, 0])
            gu = w0 * following(w0)
            gv = w0 * wn
            ue = following(u0)
            ua = jnp.where(last, ue, u0) if r >= R - H else u0
            va = jnp.where(last, vn, v0) if r >= R - H else v0
            cx[0, i, r] = gu
            cx[1, i, r] = ua * gu
            cx[2, i, r] = jnp.where(ua > 0.0, 0.5, -0.5) - 0.5 * ua
            cy[0, i, r] = gv
            cy[1, i, r] = va * gv
            cy[2, i, r] = jnp.where(va > 0.0, 0.5, -0.5) - 0.5 * va
            if r == R - H - 1:
                vf = jnp.where(last, vn, v0)
                fold[0, i] = vf * gv
                fold[1, i] = jnp.where(vf > 0.0, 0.5, -0.5) - 0.5 * vf
            a = v0 + vs
            vbar = 0.25 * (a + following(a))
            a = u0 + un
            ubar = 0.25 * (a + preceding(a))
            fu = jnp.broadcast_to(cor_u[:, r : r + 1], (8, B))
            fv = jnp.broadcast_to(cor_v[:, r : r + 1], (8, B))
            du = vbar * (fu - 0.5 * (un - us)) - 0.5 * u0 * (ue - preceding(u0))
            dv = -ubar * (fv + 0.5 * (following(v0) - preceding(v0))) - 0.5 * v0 * (vn - vs)
            new[0, i, r] = u0 + gu * du
            new[1, i, r] = v0 + gv * dv
            us, vs, u0, v0, w0 = u0, v0, un, vn, wn
        return carry

    lax.fori_loop(0, K + 1, prepare, 0)

    def merged(x, edge, k, low, high):
        if low:
            x = jnp.where(lane < low, rolled(edge, -(32 * k + 22)), x)
        return jnp.where(lane >= high, rolled(edge, 118 - 32 * k), x)

    def face(w, c, here, there, slope_here, slope_there):
        way = w > 0.0
        return w * (jnp.where(way, here, there) + c * jnp.where(way, slope_here, slope_there))

    def advect(i, carry):
        first, turned, last_jump, last_slope = [], [], [], []
        now, ahead, jump, slope, south = [], [], [], [], []
        for t in range(T):
            x0, x1 = tr[t, i, 0], tr[t, i, 1]
            xr = above(x0)
            jr = (xr - tr[t, i, R - 1]) * cy[0, i, R - 1]
            j0 = (x1 - x0) * cy[0, i, 0]
            s0 = minmod(j0, below(jr))
            turned.append(xr)
            last_jump.append(jr)
            last_slope.append(above(s0))
            now.append(x0)
            ahead.append(x1)
            jump.append(j0)
            slope.append(s0)
            south.append(None)
            first.append(None)
        for r in range(R):
            gx, wx, ex = cx[0, i, r], cx[1, i, r], cx[2, i, r]
            wy, ey = cy[1, i, r], cy[2, i, r]
            gy = cy[0, i, r + 1] if r + 1 < R - 1 else None
            for t in range(T):
                x, xn = now[t], ahead[t]
                if r + 1 < R - 1:
                    xnn = tr[t, i, r + 2]
                    jn = (xnn - xn) * gy
                    sn = minmod(jn, jump[t])
                elif r + 1 == R - 1:
                    xnn = turned[t]
                    jn = last_jump[t]
                    sn = minmod(jn, jump[t])
                else:
                    xnn = jn = None
                    sn = last_slope[t]
                north = face(wy, ey, x, xn, slope[t], sn)
                e = following(x)
                j = (e - x) * gx
                s = minmod(j, preceding(j))
                f = face(wx, ex, x, e, s, following(s))
                out = x - (f - preceding(f))
                if r == 0:
                    first[t] = out - north
                else:
                    tr[t, i, r] = out - (north - south[t])
                if r == R - H - 1:
                    north = face(fold[0, i], fold[1, i], x, xn, slope[t], sn)
                south[t] = north
                now[t], ahead[t], jump[t], slope[t] = xn, xnn, jn, sn
        for t in range(T):
            tr[t, i, 0] = first[t] + below(south[t])
        return carry

    copies[-1].wait()
    for r in range(R):
        strided = pl.ds(r, 8, stride=R)
        mix = [dext[k, strided] for k in range(K - 1)]
        gu = [merged(cx[0, k, r], cx[0, K, r], k, 0, B - 1) for k in range(K)]
        gv = [cy[0, k, r] for k in range(K)]
        un = [merged(new[0, k, r], new[0, K, r], k, 1, B - 1) for k in range(K)]
        vn = [merged(new[1, k, r], new[1, K, r], k, 1, B - 1) for k in range(K)]
        (un,) = solve([un], [mix[k] * (gu[k] * gu[k + 1]) for k in range(K - 1)])
        (vn,) = solve([vn], [mix[k] * (gv[k] * gv[k + 1]) for k in range(K - 1)])
        for k in range(K):
            ext[k, strided] = un[k]
            ext[K + k, strided] = vn[k]
    out_u = pltpu.make_async_copy(ext.at[0:K, middle], uo, store.at[0])
    out_v = pltpu.make_async_copy(ext.at[K : 2 * K, middle], vo, store.at[1])
    out_q = pltpu.make_async_copy(ext.at[2 * K :, middle], qo, store.at[2])
    out_u.start()
    out_v.start()

    for step in range(NSUB):
        lax.fori_loop(0, K + 1, advect, 0)
        if step == 0:
            for r in range(R):
                for t in range(T):
                    for k in range(K):
                        tr[t, k, r] = merged(tr[t, k, r], tr[t, K, r], k, 2, B - 2)

    for r in range(R):
        strided = pl.ds(r, 8, stride=R)
        w = [wet[k, r] for k in range(K)]
        mix = [dext[k, strided] * (w[k] * w[k + 1]) for k in range(K - 1)]
        x = [
            [merged(tr[t, k, r], tr[t, K, r], k, 4, B - 4) for k in range(K)] for t in range(T)
        ]
        for t, solved in enumerate(solve(x, mix)):
            for k in range(K):
                ext[2 * K + t * K + k, strided] = solved[k]
    out_q.start()
    out_u.wait()
    out_v.wait()
    out_q.wait()


def computed(nlat, u, v, q, m, d, halos):
    any_space = pl.BlockSpec(memory_space=pl.ANY)
    return pl.pallas_call(
        functools.partial(compute, nlat),
        out_shape=(
            jax.ShapeDtypeStruct((K, B, B), F32),
            jax.ShapeDtypeStruct((K, B, B), F32),
            jax.ShapeDtypeStruct((T * K, B, B), F32),
        ),
        in_specs=[any_space] * 11,
        out_specs=[any_space] * 3,
        scratch_shapes=[
            pltpu.VMEM(((2 + T) * K, E, B), F32),
            pltpu.VMEM((K, E, B), jnp.int32),
            pltpu.VMEM((K - 1, E, B), F32),
            pltpu.VMEM((2, 2, E, B), F32),
            pltpu.VMEM((2, K + 1, R, 8, B), F32),
            pltpu.VMEM((2, K + 1, R, 8, B), F32),
            pltpu.VMEM((T, K + 1, R, 8, B), F32),
            pltpu.VMEM((K + 1, R, 8, B), F32),
            pltpu.VMEM((3, K + 1, R, 8, B), F32),
            pltpu.VMEM((3, K + 1, R, 8, B), F32),
            pltpu.VMEM((2, K + 1, 8, B), F32),
            pltpu.SemaphoreType.DMA((11,)),
            pltpu.SemaphoreType.DMA((3,)),
        ],
        compiler_params=pltpu.CompilerParams(vmem_limit_bytes=40 * 2**20),
    )(u, v, q, m, d, *halos)


def per_device(nlat, nlon, zonal_flow, meridional_flow, tracers, sea_mask, diffusivity):
    q = tracers.reshape(T * K, B, B)
    halos = exchanged(nlat, nlon, zonal_flow, meridional_flow, q, sea_mask)
    u, v, q = computed(nlat, zonal_flow, meridional_flow, q, sea_mask, diffusivity, halos)
    return u, v, q.reshape(T, K, B, B)


def solution(mesh):
    cells = P(None, "lat", "lon")
    traced = P(None, None, "lat", "lon")
    return jax.shard_map(
        functools.partial(per_device, mesh.shape["lat"], mesh.shape["lon"]),
        mesh=mesh,
        in_specs=(cells, cells, traced, cells, cells),
        out_specs=(cells, cells, traced),
        check_vma=False,
    )
```

profile of v0, /device:TPU:30, one launch (start us, length us, event | category | flops | bytes accessed | tf_op | source)
XLA Modules:
  0.0 35.7 jit_solution(9943950090793005178)
XLA Ops:
  0.6 0.0 copy-start
  0.6 1.1 %copy-done = f32[3,4,128,128]{3,2,1,0:T(8,128)S(1)} copy-done((f32[3,4,128,128]{3,2,1,0:T(8,128)S(1)}, f32[3,4,128,128]{3,2,1,0:T(8,128)}, u32[]{:S(2)}) %copy-start) | copy-done | bytes 786456
  1.8 0.0 copy-start.2
  1.8 0.9 %copy-done.2 = f32[4,128,128]{2,1,0:T(8,128)S(1)} copy-done((f32[4,128,128]{2,1,0:T(8,128)S(1)}, f32[4,128,128]{2,1,0:T(8,128)}, u32[]{:S(2)}) %copy-start.2) | copy-done | bytes 262168
  2.7 0.0 copy-start.4
  2.7 0.9 %copy-done.4 = f32[4,128,128]{2,1,0:T(8,128)S(1)} copy-done((f32[4,128,128]{2,1,0:T(8,128)S(1)}, f32[4,128,128]{2,1,0:T(8,128)}, u32[]{:S(2)}) %copy-start.4) | copy-done | bytes 262168
  3.7 0.0 copy-start.6
  3.7 0.9 %copy-done.6 = s32[4,128,128]{2,1,0:T(8,128)S(1)} copy-done((s32[4,128,128]{2,1,0:T(8,128)S(1)}, s32[4,128,128]{2,1,0:T(8,128)}, u32[]{:S(2)}) %copy-start.6) | copy-done | bytes 262168
  4.6 0.0 copy-start.1
  4.6 0.0 copy-start.3
  4.6 0.0 copy-start.5
  4.6 0.0 copy-start.7
  4.6 17.5 %shard_map.76 = (f32[20,8,128]{2,1,0:T(8,128)S(1)}, f32[20,8,128]{2,1,0:T(8,128)S(1)}, s32[4,8,128]{2,1,0:T(8,128)S(1)}, s32[4,8,128]{2,1,0:T(8,128)S(1)}, f32[2...) custom-call(f32[4,128,128]{2,1,0:T(8,128)S(1)} %copy-done.2, f32[4,128,128]{2,1,0:T(8,128)S(1)} %copy-done.4, ...), custom_call_target="tpu_custom_call" | custom-call | tf_op jit(solution)/shard_map/pallas_call | solution.py:253
  22.1 0.0 copy-done.1
  22.2 0.0 copy-done.3
  22.2 0.0 copy-done.5
  22.2 0.0 copy-done.7
  22.2 0.0 copy-start.8
  22.2 0.9 %copy-done.8 = f32[3,128,128]{2,1,0:T(8,128)S(1)} copy-done((f32[3,128,128]{2,1,0:T(8,128)S(1)}, f32[3,128,128]{2,1,0:T(8,128)}, u32[]{:S(2)}) %copy-start.8) | copy-done | bytes 196632
  23.1 12.6 %shard_map.77 = (f32[4,128,128]{2,1,0:T(8,128)}, f32[4,128,128]{2,1,0:T(8,128)}, f32[12,128,128]{2,1,0:T(8,128)}) custom-call(f32[4,128,128]{2,1,0:T(8,128)S(1)} %copy-done.3, f32[4,128,128]{2,1,0:T(8,128)S(1)} %copy-done.5, f32[12,128,128]{2,1,0:T(8,128)S(1)} %bitcast.3, s32[4,128,128]{2,1,0:T(8,128)S(1)} %copy-done.7, f32[3,128,128]{2,1,0:T(8,128)S(1)} %copy-done.8, ...), custom_call_target="tpu_custom_call" | custom-call | tf_op jit(solution)/shard_map/pallas_call | solution.py:586
Async XLA Ops:
  0.6 1.1 %copy-start = (f32[3,4,128,128]{3,2,1,0:T(8,128)S(1)}, f32[3,4,128,128]{3,2,1,0:T(8,128)}, u32[]{:S(2)}) copy-start(f32[3,4,128,128]{3,2,1,0:T(8,128)} %param.7) | copy-start | bytes 2359300
  1.8 0.9 %copy-start.2 = (f32[4,128,128]{2,1,0:T(8,128)S(1)}, f32[4,128,128]{2,1,0:T(8,128)}, u32[]{:S(2)}) copy-start(f32[4,128,128]{2,1,0:T(8,128)} %u.3) | copy-start | bytes 786436
  2.7 0.9 %copy-start.4 = (f32[4,128,128]{2,1,0:T(8,128)S(1)}, f32[4,128,128]{2,1,0:T(8,128)}, u32[]{:S(2)}) copy-start(f32[4,128,128]{2,1,0:T(8,128)} %v.3) | copy-start | bytes 786436
  3.7 0.9 %copy-start.6 = (s32[4,128,128]{2,1,0:T(8,128)S(1)}, s32[4,128,128]{2,1,0:T(8,128)}, u32[]{:S(2)}) copy-start(s32[4,128,128]{2,1,0:T(8,128)} %m.3) | copy-start | bytes 786436
  4.6 17.5 %copy-start.1 = (f32[3,4,128,128]{3,2,1,0:T(8,128)S(1)}, f32[3,4,128,128]{3,2,1,0:T(8,128)}, u32[]{:S(2)}) copy-start(f32[3,4,128,128]{3,2,1,0:T(8,128)} %param.7) | copy-start | bytes 2359300
  4.6 17.5 %copy-start.3 = (f32[4,128,128]{2,1,0:T(8,128)S(1)}, f32[4,128,128]{2,1,0:T(8,128)}, u32[]{:S(2)}) copy-start(f32[4,128,128]{2,1,0:T(8,128)} %u.3) | copy-start | bytes 786436
  4.6 17.6 %copy-start.5 = (f32[4,128,128]{2,1,0:T(8,128)S(1)}, f32[4,128,128]{2,1,0:T(8,128)}, u32[]{:S(2)}) copy-start(f32[4,128,128]{2,1,0:T(8,128)} %v.3) | copy-start | bytes 786436
  4.6 17.6 %copy-start.7 = (s32[4,128,128]{2,1,0:T(8,128)S(1)}, s32[4,128,128]{2,1,0:T(8,128)}, u32[]{:S(2)}) copy-start(s32[4,128,128]{2,1,0:T(8,128)} %m.3) | copy-start | bytes 786436
  22.2 0.9 %copy-start.8 = (f32[3,128,128]{2,1,0:T(8,128)S(1)}, f32[3,128,128]{2,1,0:T(8,128)}, u32[]{:S(2)}) copy-start(f32[3,128,128]{2,1,0:T(8,128)} %d.1) | copy-start | bytes 589828
where the time goes:
time: 36 us; the launch traced here: 35.7 us
  Pallas kernels  30.1 us (84%)
  local copies, waits for them, and re-layouts  4.91 us (14%)
  between operations  0.7 us (2%)
    pallas_call x1, Pallas kernels, exchanged(): pl.pallas_call(functools.partial(exchange, nlat, nlon), out_shape=(jax.Sh...  17.5 us
    pallas_call x1, Pallas kernels, computed(): pl.pallas_call(functools.partial(compute, nlat), out_shape=(jax.ShapeDtyp...  12.6 us
    unnamed x18, local copies, waits for them, and re-layouts  4.91 us

commit v1 on v0

v1 whole, which is shorter than its diff:
```python
import functools
import math

import jax
import jax.numpy as jnp
from jax import lax
from jax.experimental import pallas as pl
from jax.experimental.pallas import tpu as pltpu
from jax.sharding import PartitionSpec as P

K = 4
T = 3
NSUB = 3
B = 128
H = 8
E = B + 2 * H
R = E // 8
S = 14
DEPTH = R
WET, U, V, Q = 4, 8, 12, 16
FIELDS = (WET, U, V, Q, Q + K, Q + 2 * K)
F32 = jnp.float32
MESH = pl.DeviceIdType.MESH
coriolis_peak = 0.5


def minmod(a, b):
    return jnp.maximum(jnp.minimum(a, b), jnp.minimum(jnp.maximum(a, b), 0.0))


def following(x):
    return pltpu.roll(x, B - 1, 1)


def preceding(x):
    return pltpu.roll(x, 1, 1)


def above(x):
    return pltpu.roll(x, 7, 0)


def below(x):
    return pltpu.roll(x, 1, 0)


def rolled(x, amount):
    return pltpu.roll(x, amount % B, 1) if amount % B else x


def flipped(x, index):
    x = jnp.take_along_axis(x, index, axis=1)
    backward = 7 - lax.broadcasted_iota(jnp.int32, (8, B), 0)
    return jnp.take_along_axis(x, backward, axis=0)


def solve(x, coupling):
    carried = []
    inverse = []
    for k in range(K):
        divisor = 1.0
        if k < K - 1:
            divisor = divisor + coupling[k]
        if k > 0:
            divisor = divisor + coupling[k - 1] * (1.0 - carried[k - 1])
        inverse.append(1.0 / divisor)
        if k < K - 1:
            carried.append(coupling[k] * inverse[k])
    results = []
    for field in x:
        scaled = [field[0] * inverse[0]]
        for k in range(1, K):
            scaled.append((field[k] + coupling[k - 1] * scaled[k - 1]) * inverse[k])
        solved = [scaled[K - 1]]
        for k in range(K - 2, -1, -1):
            solved.insert(0, scaled[k] + carried[k] * solved[0])
        results.append(solved)
    return results


def step(
    nlat, nlon, u, v, q, m, d, res,
    ext, mext, dext, hn, hs, hmn, hms, pe, pw, ke, kw, pn, flow, new, tr, wet, cx, cy, fold, load, send, recv,
):
    lat = lax.axis_index("lat")
    lon = lax.axis_index("lon")
    top = lat == nlat - 1
    bottom = lat == 0
    east = lax.rem(lon + 1, nlon)
    west = lax.rem(lon + nlon - 1, nlon)
    n_lat = jnp.where(top, lat, lat + 1)
    n_mid = jnp.where(top, nlon - 1 - lon, lon)
    n_west = jnp.where(top, lax.rem(nlon - lon, nlon), west)
    n_east = jnp.where(top, lax.rem(2 * nlon - 2 - lon, nlon), east)
    s_lat = jnp.maximum(lat - 1, 0)
    own_w = n_west == lon
    own_e = n_east == lon

    def at(row, column):
        return {"lat": row, "lon": column}

    middle = pl.ds(H, B)
    beyond = pl.ds(H + B, H)
    loads = [
        pltpu.make_async_copy(u, ext.at[U : U + K, middle], load.at[0]),
        pltpu.make_async_copy(v, ext.at[V : V + K, middle], load.at[1]),
        pltpu.make_async_copy(q, ext.at[Q : Q + T * K, middle], load.at[2]),
        pltpu.make_async_copy(m, mext, load.at[3]),
        pltpu.make_async_copy(d, dext.at[:, middle], load.at[4]),
    ]
    for copy in loads:
        copy.start()

    barrier = pltpu.get_barrier_semaphore()

    def greet(row, column):
        pl.semaphore_signal(barrier, inc=1, device_id=at(row, column), device_id_type=MESH)

    greet(lat, east)
    greet(lat, west)
    greet(n_lat, n_mid)

    @pl.when(jnp.logical_not(top & own_w))
    def _():
        greet(n_lat, n_west)

    @pl.when(jnp.logical_not(top & own_e))
    def _():
        greet(n_lat, n_east)

    @pl.when(jnp.logical_not(bottom))
    def _():
        greet(s_lat, lon)
        greet(s_lat, west)
        greet(s_lat, east)

    peers = (
        3
        + jnp.where(top & own_w, 0, 1)
        + jnp.where(top & own_e, 0, 1)
        + jnp.where(bottom, 0, 3)
    )
    pl.semaphore_wait(barrier, peers)

    def remote(src, dst, slot, row, column):
        return pltpu.make_async_remote_copy(
            src_ref=src,
            dst_ref=dst,
            send_sem=send.at[slot],
            recv_sem=recv.at[slot],
            device_id=at(row, column),
            device_id_type=MESH,
        )

    hi = pl.ds(B - H, H)
    lo = pl.ds(0, H)

    def rows(part, fields, marks, base, row, column):
        return [
            remote(u.at[:, part], fields.at[0:K], base, row, column),
            remote(v.at[:, part], fields.at[K : 2 * K], base + 1, row, column),
            remote(q.at[:, part], fields.at[2 * K :], base + 2, row, column),
            remote(m.at[:, part], marks, base + 3, row, column),
        ]

    to_north = rows(hi, hs, hms, 8, n_lat, n_mid)
    over_fold = rows(hi, hn, hmn, 2, n_lat, n_mid)
    to_south = rows(lo, hn, hmn, 2, s_lat, lon)

    @pl.when(top)
    def _():
        for copy in over_fold:
            copy.start()

    @pl.when(jnp.logical_not(top))
    def _():
        for copy in to_north:
            copy.start()

    @pl.when(jnp.logical_not(bottom))
    def _():
        for copy in to_south:
            copy.start()

    lane = lax.broadcasted_iota(jnp.int32, (8, B), 1)
    sub = lax.broadcasted_iota(jnp.int32, (8, B), 0)
    group = lane // 8
    for f in range(WET, Q + T * K):
        ext[f, lo] = jnp.zeros((H, B), F32)
        ext[f, beyond] = jnp.zeros((H, B), F32)
    for copy in loads:
        copy.wait()

    def pack(i, carry):
        part = pl.ds(pl.multiple_of(i * 8, 8), 8)
        held = pl.ds(pl.multiple_of(i * 8 + H, 8), 8)
        for k in range(K):
            ext[WET + k, held] = mext[k, part].astype(F32)
        for half in range(2):
            packed_w = jnp.zeros((8, B), F32)
            packed_e = jnp.zeros((8, B), F32)
            for k in range(K):
                for f, field in enumerate((Q, Q + K, Q + 2 * K, WET) if half == 0 else (U, V)):
                    x = ext[field + k, held]
                    j = 4 * k + f
                    x = pltpu.roll(x, 8 * j, 1) if j else x
                    packed_w = jnp.where(group == j, x, packed_w)
                    packed_e = jnp.where(group == (j - 1) % 16, x, packed_e)
            kw[half, part] = packed_w
            ke[half, part] = packed_e
        return carry

    lax.fori_loop(0, B // 8, pack, 0)

    sends = [
        remote(ke, pw.at[:, middle], 1, lat, east),
        remote(kw, pe.at[:, middle], 0, lat, west),
    ]
    for copy in sends:
        copy.start()
    north_east = remote(ke.at[:, hi], pw.at[:, lo], 13, n_lat, n_east)
    north_west = remote(kw.at[:, hi], pe.at[:, lo], 12, n_lat, n_west)
    fold_west = remote(kw.at[:, hi], pw.at[:, beyond], 7, n_lat, n_west)
    fold_east = remote(ke.at[:, hi], pe.at[:, beyond], 6, n_lat, n_east)
    self_west = pltpu.make_async_copy(kw.at[:, hi], pw.at[:, beyond], load.at[5])
    self_east = pltpu.make_async_copy(ke.at[:, hi], pe.at[:, beyond], load.at[6])
    south_east = remote(ke.at[:, lo], pw.at[:, beyond], 7, s_lat, east)
    south_west = remote(kw.at[:, lo], pe.at[:, beyond], 6, s_lat, west)

    @pl.when(jnp.logical_not(top))
    def _():
        north_east.start()
        north_west.start()

    @pl.when(top & own_w)
    def _():
        self_west.start()

    @pl.when(top & jnp.logical_not(own_w))
    def _():
        fold_west.start()

    @pl.when(top & own_e)
    def _():
        self_east.start()

    @pl.when(top & jnp.logical_not(own_e))
    def _():
        fold_east.start()

    @pl.when(jnp.logical_not(bottom))
    def _():
        south_east.start()
        south_west.start()

    place = lane % 32
    level = lane // 32
    far_hi = (place >= 10) & (place < 16)
    far_lo = (place >= 16) & (place < 22)
    is_hi = [(place < 10) & (level == k) for k in range(K)]
    is_lo = [(place >= 22) & (level == k) for k in range(K)]

    def edges(field, part):
        edge = jnp.zeros((8, B), F32)
        for k in range(K):
            x = ext[field + k, part]
            edge = jnp.where(is_hi[k], rolled(x, 32 * k + 10), edge)
            edge = jnp.where(is_lo[k], rolled(x, 32 * k + 22), edge)
        return edge

    def own_edges(i, carry):
        held = pl.ds(pl.multiple_of(i * 8 + H, 8), 8)
        for n, field in enumerate(FIELDS):
            pn[n, held] = edges(field, held)
        return carry

    lax.fori_loop(0, B // 8, own_edges, 0)

    def keep(n, i, r, x):
        if n == 0:
            wet[i, r] = x
        elif n < 3:
            flow[n - 1, i, r] = x
        else:
            tr[n - 3, i, r] = x

    def levels(n, r):
        for k in range(K):
            keep(n, k, r, ext[FIELDS[n] + k, pl.ds(r, 8, stride=R)])

    for r in range(R):
        for n in range(len(FIELDS)):
            levels(n, r)

    def coriolis(offset):
        row = lat * B + R * sub + lane - H
        ny = nlat * B
        return coriolis_peak * jnp.sin(math.pi * ((row.astype(F32) + offset) / ny - 0.5))

    cor_u = coriolis(0.5)
    cor_v = coriolis(1.0)

    def prepare(i, rows, count, bend, beyond_fold, momentum):
        def get(f, r):
            if r == -1:
                return below(flow[f, i, count - 1])
            if r == count:
                return above(flow[f, i, 0])
            return flow[f, i, r]

        us, vs = get(0, rows[0] - 1), get(1, rows[0] - 1)
        u0, v0 = get(0, rows[0]), get(1, rows[0])
        w0 = wet[i, rows[0]]
        for r in rows:
            un, vn = get(0, r + 1), get(1, r + 1)
            wn = wet[i, r + 1] if r < count - 1 else above(wet[i, 0])
            gu = w0 * following(w0)
            gv = w0 * wn
            ue = following(u0)
            ua = jnp.where(beyond_fold, ue, u0) if r > bend else u0
            va = jnp.where(beyond_fold, vn, v0) if r > bend else v0
            cx[0, i, r] = gu
            cx[1, i, r] = ua * gu
            cx[2, i, r] = jnp.where(ua > 0.0, 0.5, -0.5) - 0.5 * ua
            cy[0, i, r] = gv
            cy[1, i, r] = va * gv
            cy[2, i, r] = jnp.where(va > 0.0, 0.5, -0.5) - 0.5 * va
            if r == bend:
                vf = jnp.where(beyond_fold, vn, v0)
                fold[0, i] = vf * gv
                fold[1, i] = jnp.where(vf > 0.0, 0.5, -0.5) - 0.5 * vf
            if momentum:
                a = v0 + vs
                vbar = 0.25 * (a + following(a))
                a = u0 + un
                ubar = 0.25 * (a + preceding(a))
                fu = jnp.broadcast_to(cor_u[:, r : r + 1], (8, B))
                fv = jnp.broadcast_to(cor_v[:, r : r + 1], (8, B))
                du = vbar * (fu - 0.5 * (un - us)) - 0.5 * u0 * (ue - preceding(u0))
                dv = -ubar * (fv + 0.5 * (following(v0) - preceding(v0))) - 0.5 * v0 * (vn - vs)
                new[0, i, r] = u0 + gu * du
                new[1, i, r] = v0 + gv * dv
            us, vs, u0, v0, w0 = u0, v0, un, vn, wn

    last = top & (sub == 7)
    last_strip = top & (sub >= 4)
    bend = R - H - 1

    def prepare_level(rows, i, carry):
        prepare(i, rows, R, bend, last, True)
        return carry

    lax.fori_loop(0, K, functools.partial(prepare_level, range(R)), 0)

    def face(w, c, here, there, slope_here, slope_there):
        way = w > 0.0
        return w * (jnp.where(way, here, there) + c * jnp.where(way, slope_here, slope_there))

    def advect(i, count, bend):
        turned, last_jump, last_slope = [], [], []
        now, ahead, jump, slope, south = [], [], [], [], []
        for t in range(T):
            x0, x1 = tr[t, i, 0], tr[t, i, 1]
            xr = above(x0)
            jr = (xr - tr[t, i, count - 1]) * cy[0, i, count - 1]
            j0 = (x1 - x0) * cy[0, i, 0]
            s0 = minmod(j0, below(jr))
            turned.append(xr)
            last_jump.append(jr)
            last_slope.append(above(s0))
            now.append(x0)
            ahead.append(x1)
            jump.append(j0)
            slope.append(s0)
            south.append(None)
        state = {}

        def stage_a(t, r):
            x, xn = now[t], ahead[t]
            if r + 1 < count - 1:
                xnn = tr[t, i, r + 2]
                jn = (xnn - xn) * cy[0, i, r + 1]
                sn = minmod(jn, jump[t])
            elif r + 1 == count - 1:
                xnn = turned[t]
                jn = last_jump[t]
                sn = minmod(jn, jump[t])
            else:
                xnn = jn = None
                sn = last_slope[t]
            north = face(cy[1, i, r], cy[2, i, r], x, xn, slope[t], sn)
            e = following(x)
            y = x - north if r == 0 else x - (north - south[t])
            if r == bend:
                north = face(fold[0, i], fold[1, i], x, xn, slope[t], sn)
            south[t] = north
            now[t], ahead[t], jump[t], slope[t] = xn, xnn, jn, sn
            state[t, r] = (x, e, y)

        def stage_b(t, r):
            x, e, y = state[t, r]
            j = (e - x) * cx[0, i, r]
            state[t, r] = (x, e, y, j, preceding(j))

        def stage_c(t, r):
            x, e, y, j, jp = state[t, r]
            s = minmod(j, jp)
            state[t, r] = (x, e, y, s, following(s))

        def stage_d(t, r):
            x, e, y, s, sn = state[t, r]
            f = face(cx[1, i, r], cx[2, i, r], x, e, s, sn)
            state[t, r] = (y - f, preceding(f))

        def stage_e(t, r):
            y, fp = state.pop((t, r))
            y = y + fp
            tr[t, i, r] = y

        stages = [stage_a, stage_b, stage_c, stage_d, stage_e]
        for tick in range(count + 4 * DEPTH):
            for n in (4, 3, 2, 1, 0):
                r = tick - n * DEPTH
                if 0 <= r < count:
                    for t in range(T):
                        stages[n](t, r)
        for t in range(T):
            tr[t, i, 0] = tr[t, i, 0] + below(south[t])

    def advect_level(i, carry):
        advect(lax.rem(i, K + 1), R, bend)
        return carry

    def advect_inner(i, carry):
        advect(lax.rem(i, K), R, bend)
        return carry

    lax.fori_loop(0, 2 * K, advect_inner, 0)

    for copy in sends:
        copy.wait_send()

    @pl.when(top)
    def _():
        for copy in over_fold:
            copy.wait_send()

    @pl.when(jnp.logical_not(top))
    def _():
        for copy in to_north:
            copy.wait_send()
        north_east.wait_send()
        north_west.wait_send()

    @pl.when(top & own_w)
    def _():
        self_west.wait()

    @pl.when(top & jnp.logical_not(own_w))
    def _():
        fold_west.wait_send()

    @pl.when(top & own_e)
    def _():
        self_east.wait()

    @pl.when(top & jnp.logical_not(own_e))
    def _():
        fold_east.wait_send()

    @pl.when(jnp.logical_not(bottom))
    def _():
        for copy in to_south:
            copy.wait_send()
        south_east.wait_send()
        south_west.wait_send()

    for copy in sends:
        copy.wait_recv()
    for copy in to_south:
        copy.wait_recv()

    @pl.when(jnp.logical_not(top & own_w))
    def _():
        south_east.wait_recv()

    @pl.when(jnp.logical_not(top & own_e))
    def _():
        south_west.wait_recv()

    @pl.when(jnp.logical_not(bottom))
    def _():
        for copy in to_north:
            copy.wait_recv()
        north_east.wait_recv()
        north_west.wait_recv()


    for n, field in enumerate((U, V, Q, Q + K, Q + 2 * K)):
        for k in range(K):
            ext[field + k, lo] = hs[n * K + k]
            ext[field + k, beyond] = hn[n * K + k]
    for k in range(K):
        ext[WET + k, lo] = hms[k].astype(F32)
        ext[WET + k, beyond] = hmn[k].astype(F32)

    @pl.when(bottom)
    def _():
        for f in range(WET, Q + T * K):
            ext[f, lo] = jnp.zeros((H, B), F32)
        for half in range(2):
            pe[half, lo] = jnp.zeros((H, B), F32)
            pw[half, lo] = jnp.zeros((H, B), F32)

    @pl.when(top)
    def _():
        whole = B - 1 - lane
        for f in range(WET, Q + T * K):
            x = flipped(ext[f, beyond], whole)
            ext[f, beyond] = -x if U <= f < Q else x
        within = 7 - lane % 8
        from_east = (lane // 8 + 15) % 16 * 8 + within
        from_west = (lane // 8 + 1) % 16 * 8 + within
        for half in range(2):
            x = flipped(pe[half, beyond], from_east)
            pe[half, beyond] = -x if half else x
            x = flipped(pw[half, beyond], from_west)
            pw[half, beyond] = -x if half else x

    for n, field in enumerate(FIELDS):
        pn[n, lo] = edges(field, lo)
        pn[n, beyond] = edges(field, beyond)
    for i in range(R):
        part = pl.ds(8 * i, 8)
        for n in range(len(FIELDS)):
            half, slot = ((0, 3), (1, 0), (1, 1), (0, 0), (0, 1), (0, 2))[n]
            x = jnp.where(far_hi, rolled(pe[half, part], 10 - 8 * slot), pn[n, part])
            pn[n, part] = jnp.where(far_lo, rolled(pw[half, part], 22 - 8 * slot), x)
    for r in range(R):
        for n in range(len(FIELDS)):
            keep(n, K, r, pn[n, pl.ds(r, 8, stride=R)])

    flat = ext.reshape(32 * E, B)
    for r in range(S):
        for n, field in enumerate(FIELDS):
            south_rows = flat[pl.ds(field * E + H - 6 + r, 8, stride=E), :]
            north_rows = flat[pl.ds((field - K) * E + H + 120 + r, 8, stride=E), :]
            keep(n, K + 1, r, jnp.where(sub < 4, south_rows, north_rows))

    for r in (6, 7, 10, 11):
        for n in range(3):
            levels(n, r)
    prepare(K, range(R), R, bend, last, True)
    prepare(K + 1, range(S), S, 7, last_strip, False)
    lax.fori_loop(0, K, functools.partial(prepare_level, range(6, 11)), 0)

    def advect_edges(i, carry):
        advect(K, R, bend)
        advect(K + 1, S, 7)
        return carry

    lax.fori_loop(0, 2, advect_edges, 0)

    def merged(x, edge, k, low, high):
        source = jnp.where(lane < B // 2, lane + 32 * k + 22, lane + 32 * k + 10) % B
        edge = jnp.take_along_axis(edge, source, axis=1)
        return jnp.where((lane < low) | (lane >= high), edge, x)

    ends = (sub == 0) | (sub == 7)
    for t in range(T):
        for k in range(K):
            source = jnp.where(sub == 0, k, 4 + k)
            for r in range(R):
                x = tr[t, k, r]
                if 6 <= r < 12:
                    x = jnp.where(ends, jnp.take_along_axis(tr[t, K + 1, r - 2], source, axis=0), x)
                tr[t, k, r] = merged(x, tr[t, K, r], k, 4, B - 4)

    lax.fori_loop(0, K + 1, advect_level, 0)

    for r in range(R):
        strided = pl.ds(r, 8, stride=R)
        mix = [dext[k, strided] for k in range(K - 1)]
        gu = [merged(cx[0, k, r], cx[0, K, r], k, 0, B - 1) for k in range(K)]
        gv = [cy[0, k, r] for k in range(K)]
        un = [merged(new[0, k, r], new[0, K, r], k, 1, B - 1) for k in range(K)]
        vn = [merged(new[1, k, r], new[1, K, r], k, 1, B - 1) for k in range(K)]
        (un,) = solve([un], [mix[k] * (gu[k] * gu[k + 1]) for k in range(K - 1)])
        (vn,) = solve([vn], [mix[k] * (gv[k] * gv[k + 1]) for k in range(K - 1)])
        for k in range(K):
            res[k, strided] = un[k]
            res[K + k, strided] = vn[k]
        w = [wet[k, r] for k in range(K)]
        mix = [mix[k] * (w[k] * w[k + 1]) for k in range(K - 1)]
        x = [
            [merged(tr[t, k, r], tr[t, K, r], k, 2, B - 2) for k in range(K)] for t in range(T)
        ]
        for t, solved in enumerate(solve(x, mix)):
            for k in range(K):
                res[2 * K + t * K + k, strided] = solved[k]


def stepped(nlat, nlon, u, v, q, m, d):
    hbm = pl.BlockSpec(memory_space=pltpu.HBM)
    return pl.pallas_call(
        functools.partial(step, nlat, nlon),
        out_shape=jax.ShapeDtypeStruct(((2 + T) * K, E, B), F32),
        in_specs=[hbm] * 5,
        out_specs=pl.BlockSpec(memory_space=pltpu.VMEM),
        scratch_shapes=[
            pltpu.VMEM((32, E, B), F32),
            pltpu.VMEM((K, B, B), jnp.int32),
            pltpu.VMEM((K - 1, E, B), F32),
            pltpu.VMEM(((2 + T) * K, H, B), F32),
            pltpu.VMEM(((2 + T) * K, H, B), F32),
            pltpu.VMEM((K, H, B), jnp.int32),
            pltpu.VMEM((K, H, B), jnp.int32),
            pltpu.VMEM((2, E, B), F32),
            pltpu.VMEM((2, E, B), F32),
            pltpu.VMEM((2, B, B), F32),
            pltpu.VMEM((2, B, B), F32),
            pltpu.VMEM((len(FIELDS), E, B), F32),
            pltpu.VMEM((2, K + 2, R, 8, B), F32),
            pltpu.VMEM((2, K + 1, R, 8, B), F32),
            pltpu.VMEM((T, K + 2, R, 8, B), F32),
            pltpu.VMEM((K + 2, R, 8, B), F32),
            pltpu.VMEM((3, K + 2, R, 8, B), F32),
            pltpu.VMEM((3, K + 2, R, 8, B), F32),
            pltpu.VMEM((2, K + 2, 8, B), F32),
            pltpu.SemaphoreType.DMA((7,)),
            pltpu.SemaphoreType.DMA((14,)),
            pltpu.SemaphoreType.DMA((14,)),
        ],
        compiler_params=pltpu.CompilerParams(
            collective_id=0, has_side_effects=True, vmem_limit_bytes=40 * 2**20
        ),
    )(u, v, q, m, d)


def deliver(res, u, v, q, done):
    middle = pl.ds(H, B)
    copies = [
        pltpu.make_async_copy(res.at[0:K, middle], u, done.at[0]),
        pltpu.make_async_copy(res.at[K : 2 * K, middle], v, done.at[1]),
        pltpu.make_async_copy(res.at[2 * K :, middle], q, done.at[2]),
    ]
    for copy in copies:
        copy.start()
    for copy in copies:
        copy.wait()


def delivered(res):
    return pl.pallas_call(
        deliver,
        out_shape=(
            jax.ShapeDtypeStruct((K, B, B), F32),
            jax.ShapeDtypeStruct((K, B, B), F32),
            jax.ShapeDtypeStruct((T * K, B, B), F32),
        ),
        in_specs=[pl.BlockSpec(memory_space=pltpu.VMEM)],
        out_specs=[pl.BlockSpec(memory_space=pltpu.HBM)] * 3,
        scratch_shapes=[pltpu.SemaphoreType.DMA((3,))],
    )(res)


def per_device(nlat, nlon, zonal_flow, meridional_flow, tracers, sea_mask, diffusivity):
    q = tracers.reshape(T * K, B, B)
    given = [
        pltpu.with_memory_space_constraint(x, pltpu.HBM)
        for x in (zonal_flow, meridional_flow, q, sea_mask, diffusivity)
    ]
    res = pltpu.with_memory_space_constraint(stepped(nlat, nlon, *given), pltpu.VMEM)
    u, v, q = delivered(res)
    return u, v, q.reshape(T, K, B, B)


def solution(mesh):
    cells = P(None, "lat", "lon")
    traced = P(None, None, "lat", "lon")
    return jax.shard_map(
        functools.partial(per_device, mesh.shape["lat"], mesh.shape["lon"]),
        mesh=mesh,
        in_specs=(cells, cells, traced, cells, cells),
        out_specs=(cells, cells, traced),
        check_vma=False,
    )
```

time: 36 us -> 25.3 us (0.70)
  Pallas kernels: 30.1 us -> 24.6 us
  local copies, waits for them, and re-layouts: 4.91 us -> 0 us
    pallas_call x2, Pallas kernels: 30.1 us -> 24.6 us  [the longest x1 23.5 us: stepped(): pl.pallas_call(functools.partial(step, nlat, nlon), out_shape=jax.ShapeDt...]
    unnamed x18 -> x0, local copies, waits for them, and re-layouts: 4.91 us -> none
where the time goes in v1:
time: 25.3 us; the launch traced here: 25.2 us
  Pallas kernels  24.6 us (97%)
  between operations  0.64 us (3%)
    pallas_call x1, Pallas kernels, stepped(): pl.pallas_call(functools.partial(step, nlat, nlon), out_shape=jax.ShapeDt...  23.5 us
    pallas_call x1, Pallas kernels, delivered(): pl.pallas_call(deliver, out_shape=(jax.ShapeDtypeStruct((K, B, B), F32),...  1.08 us

profile of v1, /device:TPU:30, one launch (start us, length us, event | category | flops | bytes accessed | tf_op | source)
XLA Modules:
  0.0 25.2 jit_solution(12030423783978742880)
XLA Ops:
  0.6 23.5 %shard_map.76.res = f32[20,144,128]{2,1,0:T(8,128)S(1)} custom-call(f32[4,128,128]{2,1,0:T(8,128)} %u.1, f32[4,128,128]{2,1,0:T(8,128)} %v.1, f32[12,128,128]{2,1,0:T(8,128)} %bitcast.2, s32[4,128,128]{2,1,0:T(8,128)} %m.1, f32[3,128,128]{2,1,0:T(8,128)} %d.1), custom_call_target="tpu_custom_call" | custom-call | tf_op jit(solution)/shard_map/pallas_call | solution.py:605
  24.1 1.1 %shard_map.77 = (f32[4,128,128]{2,1,0:T(8,128)}, f32[4,128,128]{2,1,0:T(8,128)}, f32[12,128,128]{2,1,0:T(8,128)}) custom-call(f32[20,144,128]{2,1,0:T(8,128)S(1)} %shard_map.76.res), custom_call_target="tpu_custom_call" | custom-call | tf_op jit(solution)/shard_map/pallas_call | solution.py:654

commit v2 on v1

v2 whole, which is shorter than its diff:
```python
import functools
import math

import jax
import jax.numpy as jnp
from jax import lax
from jax.experimental import pallas as pl
from jax.experimental.pallas import tpu as pltpu
from jax.sharding import PartitionSpec as P

K = 4
T = 3
NSUB = 3
B = 128
H = 8
E = B + 2 * H
R = E // 8
S = 14
DEPTH = R
WET, U, V, Q = 4, 8, 12, 16
FIELDS = (WET, U, V, Q, Q + K, Q + 2 * K)
F32 = jnp.float32
MESH = pl.DeviceIdType.MESH
coriolis_peak = 0.5


def flush(pending):
    for ref, index, x in pending:
        ref[index] = x
    pending.clear()


class Batch:
    def __init__(self, parts):
        self.parts = list(parts)

    def __add__(self, other):
        return each(jnp.add, self, other)

    __radd__ = __add__

    def __sub__(self, other):
        return each(jnp.subtract, self, other)

    def __rsub__(self, other):
        return each(jnp.subtract, other, self)

    def __mul__(self, other):
        return each(jnp.multiply, self, other)

    __rmul__ = __mul__

    def __rtruediv__(self, other):
        return each(jnp.divide, other, self)

    def __neg__(self):
        return each(jnp.negative, self)

    def __gt__(self, other):
        return each(jnp.greater, self, other)


def each(function, *given):
    size = [len(x.parts) for x in given if isinstance(x, Batch)]
    if not size:
        return function(*given)
    return Batch(
        function(*(x.parts[n] if isinstance(x, Batch) else x for x in given)) for n in range(size[0])
    )


def where(mask, a, b):
    return each(jnp.where, mask, a, b)


def minmod(a, b):
    return each(jnp.maximum, each(jnp.minimum, a, b), each(jnp.minimum, each(jnp.maximum, a, b), 0.0))


def following(x):
    return each(lambda part: pltpu.roll(part, B - 1, 1), x)


def preceding(x):
    return each(lambda part: pltpu.roll(part, 1, 1), x)


def above(x):
    return pltpu.roll(x, 7, 0)


def below(x):
    return pltpu.roll(x, 1, 0)


def rolled(x, amount):
    return each(lambda part: pltpu.roll(part, amount % B, 1), x) if amount % B else x


def picked(x, index):
    return each(lambda part: jnp.take_along_axis(part, index, axis=1), x)


def flipped(x, index):
    x = jnp.take_along_axis(x, index, axis=1)
    backward = 7 - lax.broadcasted_iota(jnp.int32, (8, B), 0)
    return jnp.take_along_axis(x, backward, axis=0)


def solve(x, coupling):
    carried = []
    inverse = []
    for k in range(K):
        divisor = 1.0
        if k < K - 1:
            divisor = divisor + coupling[k]
        if k > 0:
            divisor = divisor + coupling[k - 1] * (1.0 - carried[k - 1])
        inverse.append(1.0 / divisor)
        if k < K - 1:
            carried.append(coupling[k] * inverse[k])
    results = []
    for field in x:
        scaled = [field[0] * inverse[0]]
        for k in range(1, K):
            scaled.append((field[k] + coupling[k - 1] * scaled[k - 1]) * inverse[k])
        solved = [scaled[K - 1]]
        for k in range(K - 2, -1, -1):
            solved.insert(0, scaled[k] + carried[k] * solved[0])
        results.append(solved)
    return results


def step(
    nlat, nlon, u, v, q, m, d, res,
    ext, mext, dext, hn, hs, hmn, hms, pe, pw, ke, kw, pn, flow, new, tr, wet, cx, cy, fold, cor, load, send, recv,
):
    lat = lax.axis_index("lat")
    lon = lax.axis_index("lon")
    top = lat == nlat - 1
    bottom = lat == 0
    east = lax.rem(lon + 1, nlon)
    west = lax.rem(lon + nlon - 1, nlon)
    n_lat = jnp.where(top, lat, lat + 1)
    n_mid = jnp.where(top, nlon - 1 - lon, lon)
    n_west = jnp.where(top, lax.rem(nlon - lon, nlon), west)
    n_east = jnp.where(top, lax.rem(2 * nlon - 2 - lon, nlon), east)
    s_lat = jnp.maximum(lat - 1, 0)
    own_w = n_west == lon
    own_e = n_east == lon

    def at(row, column):
        return {"lat": row, "lon": column}

    middle = pl.ds(H, B)
    beyond = pl.ds(H + B, H)
    loads = [
        pltpu.make_async_copy(u, ext.at[U : U + K, middle], load.at[0]),
        pltpu.make_async_copy(v, ext.at[V : V + K, middle], load.at[1]),
        pltpu.make_async_copy(q, ext.at[Q : Q + T * K, middle], load.at[2]),
        pltpu.make_async_copy(m, mext, load.at[3]),
        pltpu.make_async_copy(d, dext.at[:, middle], load.at[4]),
    ]
    for copy in loads:
        copy.start()

    barrier = pltpu.get_barrier_semaphore()

    def greet(row, column):
        pl.semaphore_signal(barrier, inc=1, device_id=at(row, column), device_id_type=MESH)

    greet(lat, east)
    greet(lat, west)
    greet(n_lat, n_mid)

    @pl.when(jnp.logical_not(top & own_w))
    def _():
        greet(n_lat, n_west)

    @pl.when(jnp.logical_not(top & own_e))
    def _():
        greet(n_lat, n_east)

    @pl.when(jnp.logical_not(bottom))
    def _():
        greet(s_lat, lon)
        greet(s_lat, west)
        greet(s_lat, east)

    def remote(src, dst, slot, row, column):
        return pltpu.make_async_remote_copy(
            src_ref=src,
            dst_ref=dst,
            send_sem=send.at[slot],
            recv_sem=recv.at[slot],
            device_id=at(row, column),
            device_id_type=MESH,
        )

    hi = pl.ds(B - H, H)
    lo = pl.ds(0, H)
    lo_held = pl.ds(H, H)
    hi_held = pl.ds(B, H)

    def rows(part, fields, marks, base, row, column):
        return [
            remote(u.at[:, part], fields.at[0:K], base, row, column),
            remote(v.at[:, part], fields.at[K : 2 * K], base + 1, row, column),
            remote(q.at[:, part], fields.at[2 * K :], base + 2, row, column),
            remote(m.at[:, part], marks, base + 3, row, column),
        ]

    to_north = rows(hi, hs, hms, 8, n_lat, n_mid)
    over_fold = rows(hi, hn, hmn, 2, n_lat, n_mid)
    to_south = rows(lo, hn, hmn, 2, s_lat, lon)

    def enter():
        peers = (
            3
            + jnp.where(top & own_w, 0, 1)
            + jnp.where(top & own_e, 0, 1)
            + jnp.where(bottom, 0, 3)
        )
        pl.semaphore_wait(barrier, peers)

        @pl.when(top)
        def _():
            for copy in over_fold:
                copy.start()

        @pl.when(jnp.logical_not(top))
        def _():
            for copy in to_north:
                copy.start()

        @pl.when(jnp.logical_not(bottom))
        def _():
            for copy in to_south:
                copy.start()

    reached_late = lon >= nlon // 2

    @pl.when(reached_late)
    def _():
        enter()

    lane = lax.broadcasted_iota(jnp.int32, (8, B), 1)
    sub = lax.broadcasted_iota(jnp.int32, (8, B), 0)
    group = lane // 8
    own_rows, lo_pack, hi_pack = pl.ds(H, B), pl.ds(0, 2 * H), pl.ds(B, 2 * H)
    lo_land, mid_land, hi_land = pl.ds(0, 2 * H), pl.ds(2 * H, B), pl.ds(2 * H + B, 2 * H)
    sends = [
        remote(ke.at[own_rows], pw.at[mid_land], 1, lat, east),
        remote(kw.at[own_rows], pe.at[mid_land], 0, lat, west),
    ]
    north_east = remote(ke.at[hi_pack], pw.at[lo_land], 13, n_lat, n_east)
    north_west = remote(kw.at[hi_pack], pe.at[lo_land], 12, n_lat, n_west)
    fold_west = remote(kw.at[hi_pack], pw.at[hi_land], 7, n_lat, n_west)
    fold_east = remote(ke.at[hi_pack], pe.at[hi_land], 6, n_lat, n_east)
    self_west = pltpu.make_async_copy(kw.at[hi_pack], pw.at[hi_land], load.at[5])
    self_east = pltpu.make_async_copy(ke.at[hi_pack], pe.at[hi_land], load.at[6])
    south_east = remote(ke.at[lo_pack], pw.at[hi_land], 7, s_lat, east)
    south_west = remote(kw.at[lo_pack], pe.at[hi_land], 6, s_lat, west)

    for f in range(WET, Q + T * K):
        ext[f, lo] = jnp.zeros((H, B), F32)
        ext[f, beyond] = jnp.zeros((H, B), F32)
    for copy in loads:
        copy.wait()

    place = lane % 32
    level = lane // 32
    spare_w = (place == 6) | (place == 7) | (place == 14) | (place == 15)
    spare_e = (place == 0) | (place == 1) | (place == 8) | (place == 9)
    spare_of = jnp.where(
        spare_w,
        jnp.where(place < 8, place - 6, place - 12),
        jnp.where(place < 8, B - 4 + place, B - 10 + place),
    )
    spare_of = jnp.minimum(spare_of, B - 1)

    blocks = [pl.ds(i * 8, 8) for i in range(B // 8)]
    held_blocks = [pl.ds(i * 8 + H, 8) for i in range(B // 8)]

    def read(ref, *index):
        return Batch(ref[(*index, part)] for part in held_blocks)

    pending = []

    def write(ref, index, x):
        for part, y in zip(held_blocks, x.parts, strict=True):
            pending.append((ref, (*index, part), y))

    packed_w = packed_e = Batch([jnp.zeros((8, B), F32)] * len(blocks))
    for k in range(K):
        sea = Batch(mext[k, part].astype(F32) for part in blocks)
        write(ext, (WET + k,), sea)
        for f in range(T + 1):
            j = 4 * k + f
            x = rolled(read(ext, Q + f * K + k) if f < T else sea, 8 * j)
            packed_w = where(group == j, x, packed_w)
            packed_e = where(group == (j - 1) % 16, x, packed_e)
        x = picked(read(ext, V + k), spare_of)
        packed_w = where(spare_w & (level == k), x, packed_w)
        packed_e = where(spare_e & (level == k), x, packed_e)
    write(kw, (), packed_w)
    write(ke, (), packed_e)
    flush(pending)
    for first, held in ((0, lo_held), (B + H, hi_held)):
        packed_w = jnp.zeros((8, B), F32)
        packed_e = jnp.zeros((8, B), F32)
        for k in range(K):
            for f, field in enumerate((U, V)):
                j = 4 * k + f
                x = rolled(ext[field + k, held], 8 * j)
                packed_w = jnp.where(group == j, x, packed_w)
                packed_e = jnp.where(group == (j - 1) % 16, x, packed_e)
        kw[pl.ds(first, 8)] = packed_w
        ke[pl.ds(first, 8)] = packed_e

    def enter_columns():
        @pl.when(jnp.logical_not(top))
        def _():
            north_east.start()
            north_west.start()

        @pl.when(top & own_w)
        def _():
            self_west.start()

        @pl.when(top & jnp.logical_not(own_w))
        def _():
            fold_west.start()

        @pl.when(top & own_e)
        def _():
            self_east.start()

        @pl.when(top & jnp.logical_not(own_e))
        def _():
            fold_east.start()

        @pl.when(jnp.logical_not(bottom))
        def _():
            south_east.start()
            south_west.start()

        for copy in sends:
            copy.start()

    @pl.when(reached_late)
    def _():
        enter_columns()

    far_hi = (place >= 10) & (place < 16)
    far_lo = (place >= 16) & (place < 22)
    source_of = (place + jnp.where(place < 16, 118, B - 22)) % B

    def edges(field, parts):
        edge = picked(Batch(ext[field, part] for part in parts), source_of)
        for k in range(1, K):
            x = picked(Batch(ext[field + k, part] for part in parts), source_of)
            edge = where(level == k, x, edge)
        return edge

    for n, field in enumerate(FIELDS):
        write(pn, (n,), edges(field, held_blocks))
        flush(pending)

    def keep(n, i, r, x):
        ref, index = (wet, (i, r)) if n == 0 else (flow, (n - 1, i, r)) if n < 3 else (tr, (n - 3, i, r))
        pending.append((ref, index, x))

    def levels(n, r):
        for k in range(K):
            keep(n, k, r, ext[FIELDS[n] + k, pl.ds(r, 8, stride=R)])

    for r in range(R):
        for n in range(len(FIELDS)):
            levels(n, r)
        flush(pending)

    @pl.when(jnp.logical_not(reached_late))
    def _():
        enter()
        enter_columns()

    def coriolis(offset):
        row = lat * B + R * sub + lane - H
        ny = nlat * B
        return coriolis_peak * jnp.sin(math.pi * ((row.astype(F32) + offset) / ny - 0.5))

    for f, offset in enumerate((0.5, 1.0)):
        turning = coriolis(offset)
        for r in range(R):
            cor[f, r] = jnp.broadcast_to(turning[:, r : r + 1], (8, B))

    def prepare(i, rows, count, bend, beyond_fold, momentum):
        def get(f, r):
            if r == -1:
                return below(flow[f, i, count - 1])
            if r == count:
                return above(flow[f, i, 0])
            return flow[f, i, r]

        for start in range(0, len(rows), 9):
            chunk = rows[start : start + 9]

            def put(ref, index, x):
                for r, y in zip(chunk, x.parts, strict=True):
                    held_back.append((ref, (index, i, r), y))

            def bent(a, b):
                return Batch(
                    jnp.where(beyond_fold, x, y) if r > bend else y
                    for r, x, y in zip(chunk, a.parts, b.parts, strict=True)
                )

            held_back = []
            u0, v0 = (Batch(get(f, r) for r in chunk) for f in range(2))
            un, vn = (Batch(get(f, r + 1) for r in chunk) for f in range(2))
            w0 = Batch(wet[i, r] for r in chunk)
            wn = Batch(wet[i, r + 1] if r < count - 1 else above(wet[i, 0]) for r in chunk)
            gu = w0 * following(w0)
            gv = w0 * wn
            ue = following(u0)
            uw = preceding(u0)
            gw = preceding(gu)
            ua = bent(ue, u0)
            wa = bent(u0, uw)
            va = bent(vn, v0)
            put(cx, 0, gu)
            put(cx, 1, each(jnp.maximum, ua, 0.0) * gu)
            put(cx, 2, 0.5 - 0.5 * ua)
            put(cx, 3, gw)
            put(cx, 4, each(jnp.minimum, wa, 0.0) * gw)
            put(cx, 5, -0.5 - 0.5 * wa)
            put(cy, 0, gv)
            put(cy, 1, va * gv)
            put(cy, 2, where(va > 0.0, 0.5, -0.5) - 0.5 * va)
            if bend in chunk:
                n = chunk.index(bend)
                vf = jnp.where(beyond_fold, vn.parts[n], v0.parts[n])
                held_back.append((fold, (0, i), vf * gv.parts[n]))
                held_back.append((fold, (1, i), jnp.where(vf > 0.0, 0.5, -0.5) - 0.5 * vf))
            if momentum:
                us, vs = (Batch(get(f, r - 1) for r in chunk) for f in range(2))
                turn_u, turn_v = (Batch(cor[f, r] for r in chunk) for f in range(2))
                a = v0 + vs
                vbar = 0.25 * (a + following(a))
                a = u0 + un
                ubar = 0.25 * (a + preceding(a))
                du = vbar * (turn_u - 0.5 * (un - us)) - 0.5 * u0 * (ue - uw)
                dv = -ubar * (turn_v + 0.5 * (following(v0) - preceding(v0))) - 0.5 * v0 * (vn - vs)
                put(new, 0, u0 + gu * du)
                put(new, 1, v0 + gv * dv)
            flush(held_back)

    last = top & (sub == 7)
    last_strip = top & (sub >= 4)
    bend = R - H - 1

    def prepare_level(rows, i, carry):
        prepare(i, rows, R, bend, last, True)
        return carry

    lax.fori_loop(0, K, functools.partial(prepare_level, range(R)), 0)

    def face(w, c, here, there, slope_here, slope_there):
        way = w > 0.0
        return w * (jnp.where(way, here, there) + c * jnp.where(way, slope_here, slope_there))

    def advect(i, count, bend):
        first, held_back = [None] * T, []
        turned, last_jump, last_slope = [], [], []
        now, ahead, jump, slope, south = [], [], [], [], []
        for t in range(T):
            x0, x1 = tr[t, i, 0], tr[t, i, 1]
            xr = above(x0)
            jr = (xr - tr[t, i, count - 1]) * cy[0, i, count - 1]
            j0 = (x1 - x0) * cy[0, i, 0]
            s0 = minmod(j0, below(jr))
            turned.append(xr)
            last_jump.append(jr)
            last_slope.append(above(s0))
            now.append(x0)
            ahead.append(x1)
            jump.append(j0)
            slope.append(s0)
            south.append(None)
        state = {}

        def stage_a(t, r):
            x = tr[t, i, r]
            state[t, r] = (following(x), preceding(x))

        def stage_b(t, r):
            e, p = state[t, r]
            x = tr[t, i, r]
            s = minmod((e - x) * cx[0, i, r], (x - p) * cx[3, i, r])
            a = cx[1, i, r] * (x + cx[2, i, r] * s)
            b = cx[4, i, r] * (x + cx[5, i, r] * s)
            state[t, r] = (b - a, preceding(a), following(b))

        def stage_e(t, r):
            own, a, b = state.pop((t, r))
            x, xn = now[t], ahead[t]
            if r + 1 < count - 1:
                xnn = tr[t, i, r + 2]
                jn = (xnn - xn) * cy[0, i, r + 1]
                sn = minmod(jn, jump[t])
            elif r + 1 == count - 1:
                xnn = turned[t]
                jn = last_jump[t]
                sn = minmod(jn, jump[t])
            else:
                xnn = jn = None
                sn = last_slope[t]
            north = face(cy[1, i, r], cy[2, i, r], x, xn, slope[t], sn)
            y = x - north if r == 0 else x - (north - south[t])
            if r == bend:
                north = face(fold[0, i], fold[1, i], x, xn, slope[t], sn)
            south[t] = north
            now[t], ahead[t], jump[t], slope[t] = xn, xnn, jn, sn
            y = y + (own + (a - b))
            if r == 0:
                first[t] = y
            else:
                held_back.append((tr, (t, i, r), y))

        stages = [stage_a, stage_b, stage_e]
        for tick in range(count + 2 * DEPTH):
            for n in (2, 1, 0):
                r = tick - n * DEPTH
                if 0 <= r < count:
                    for t in range(T):
                        stages[n](t, r)
            if tick % 3 == 2:
                flush(held_back)
        flush(held_back)
        for t in range(T):
            tr[t, i, 0] = first[t] + below(south[t])

    def advect_level(i, carry):
        advect(lax.rem(i, K + 1), R, bend)
        return carry

    def advect_inner(i, carry):
        advect(lax.rem(i, K), R, bend)
        return carry

    lax.fori_loop(0, 2 * K, advect_inner, 0)

    for copy in sends:
        copy.wait_send()

    @pl.when(top)
    def _():
        for copy in over_fold:
            copy.wait_send()

    @pl.when(jnp.logical_not(top))
    def _():
        for copy in to_north:
            copy.wait_send()
        north_east.wait_send()
        north_west.wait_send()

    @pl.when(top & own_w)
    def _():
        self_west.wait()

    @pl.when(top & jnp.logical_not(own_w))
    def _():
        fold_west.wait_send()

    @pl.when(top & own_e)
    def _():
        self_east.wait()

    @pl.when(top & jnp.logical_not(own_e))
    def _():
        fold_east.wait_send()

    @pl.when(jnp.logical_not(bottom))
    def _():
        for copy in to_south:
            copy.wait_send()
        south_east.wait_send()
        south_west.wait_send()

    for copy in sends:
        copy.wait_recv()
    for copy in to_south:
        copy.wait_recv()

    @pl.when(jnp.logical_not(top & own_w))
    def _():
        south_east.wait_recv()

    @pl.when(jnp.logical_not(top & own_e))
    def _():
        south_west.wait_recv()

    @pl.when(jnp.logical_not(bottom))
    def _():
        for copy in to_north:
            copy.wait_recv()
        north_east.wait_recv()
        north_west.wait_recv()


    for n, field in enumerate((U, V, Q, Q + K, Q + 2 * K)):
        for k in range(K):
            pending.append((ext, (field + k, lo), hs[n * K + k]))
            pending.append((ext, (field + k, beyond), hn[n * K + k]))
    for k in range(K):
        pending.append((ext, (WET + k, lo), hms[k].astype(F32)))
        pending.append((ext, (WET + k, beyond), hmn[k].astype(F32)))
    flush(pending)

    @pl.when(bottom)
    def _():
        for f in range(WET, Q + T * K):
            ext[f, lo] = jnp.zeros((H, B), F32)
        pe[lo_land] = jnp.zeros((2 * H, B), F32)
        pw[lo_land] = jnp.zeros((2 * H, B), F32)

    @pl.when(top)
    def _():
        whole = B - 1 - lane
        turned = [flipped(ext[f, beyond], whole) for f in range(WET, Q + T * K)]
        for f, x in enumerate(turned, WET):
            ext[f, beyond] = -x if U <= f < Q else x
        within = 7 - lane % 8
        from_east = (lane // 8 + 15) % 16 * 8 + within
        from_west = (lane // 8 + 1) % 16 * 8 + within
        first, second = pl.ds(2 * H + B, H), pl.ds(3 * H + B, H)
        for landed, source in ((pe, from_east), (pw, from_west)):
            x, y = flipped(landed[first], source), flipped(landed[second], source)
            landed[first] = -y
            landed[second] = x

    def spread(n, parts, pack_e, pack_w, slot, own):
        x = where(far_hi, rolled(pack_e, 10 - 8 * slot), own)
        x = where(far_lo, rolled(pack_w, 22 - 8 * slot), x)
        for part, y in zip(parts, x.parts, strict=True):
            pending.append((pn, (n, part), y))

    corners = ((lo, beyond), (lo, pl.ds(3 * H + B, H)), (pl.ds(H, H), pl.ds(2 * H + B, H)))
    for n, slot in ((0, 3), (3, 0), (4, 1), (5, 2), (1, 0), (2, 1)):
        landed = corners[2] if n in (1, 2) else corners[1]
        pack_e, pack_w = (Batch(pack[part] for part in landed) for pack in (pe, pw))
        spread(n, corners[0], pack_e, pack_w, slot, edges(FIELDS[n], corners[0]))
    landed = [pl.ds(i * 8 + 2 * H, 8) for i in range(B // 8)]
    pack_e, pack_w = (Batch(pack[part] for part in landed) for pack in (pe, pw))
    for n, slot in ((0, 3), (3, 0), (4, 1), (5, 2)):
        spread(n, held_blocks, pack_e, pack_w, slot, read(pn, n))
    from_spare_e = jnp.where(place < 12, lane - 4, lane + 2)
    from_spare_w = jnp.where(place < 20, lane - 18, lane - 12)
    from_spare = jnp.where(place < 16, from_spare_e, from_spare_w) % B
    x = where(far_hi, picked(pack_e, from_spare), read(pn, 2))
    far_v = where(far_lo, picked(pack_w, from_spare), x)
    write(pn, (2,), far_v)
    flush(pending)
    run_hi = (place >= 9) & (place < 14)
    run_lo = (place >= 17) & (place < 23)
    own = read(pn, 1)
    dv = far_v - Batch(pn[2, pl.ds(i * 8 + H - 1, 8)] for i in range(B // 8))
    x = where(run_hi, where(place == 9, own, -dv), 0.0)
    y = where(run_lo, where(place == 22, own, rolled(dv, -1)), 0.0)
    x2, y2 = x + rolled(x, 1), y + rolled(y, -1)
    x, y = x2 + rolled(x2, 2) + rolled(x, 4), y2 + rolled(y2, -2) + rolled(y2, -4)
    write(pn, (1,), where(far_hi, x, where(far_lo, y, own)))
    flush(pending)
    for r in range(R):
        for n in range(len(FIELDS)):
            keep(n, K, r, pn[n, pl.ds(r, 8, stride=R)])
        flush(pending)

    flat = ext.reshape(32 * E, B)
    for r in range(S):
        for n, field in enumerate(FIELDS):
            south_rows = flat[pl.ds(field * E + H - 6 + r, 8, stride=E), :]
            north_rows = flat[pl.ds((field - K) * E + H + 120 + r, 8, stride=E), :]
            keep(n, K + 1, r, jnp.where(sub < 4, south_rows, north_rows))
        flush(pending)

    for r in (6, 7, 10, 11):
        for n in range(3):
            levels(n, r)
        flush(pending)
    prepare(K, range(R), R, bend, last, True)
    prepare(K + 1, range(S), S, 7, last_strip, False)
    lax.fori_loop(0, K, functools.partial(prepare_level, range(6, 11)), 0)

    def advect_edges(i, carry):
        advect(K, R, bend)
        advect(K + 1, S, 7)
        return carry

    lax.fori_loop(0, 2, advect_edges, 0)

    def merged(x, edge, k, low, high):
        source = jnp.where(lane < B // 2, lane + 32 * k + 22, lane + 32 * k + 10) % B
        return where((lane < low) | (lane >= high), picked(edge, source), x)

    ends = (sub == 0) | (sub == 7)
    for t in range(T):
        for k in range(K):
            source = jnp.where(sub == 0, k, 4 + k)
            x = [tr[t, k, r] for r in range(R)]
            for r in range(6, 12):
                x[r] = jnp.where(ends, jnp.take_along_axis(tr[t, K + 1, r - 2], source, axis=0), x[r])
            x = merged(Batch(x), Batch(tr[t, K, r] for r in range(R)), k, 4, B - 4)
            for r in range(R):
                pending.append((tr, (t, k, r), x.parts[r]))
            flush(pending)

    lax.fori_loop(0, K + 1, advect_level, 0)

    for start in range(0, R, 6):
        strided = [pl.ds(r, 8, stride=R) for r in range(start, start + 6)]

        def rows_of(ref, *index):
            return Batch(ref[(*index, r)] for r in range(start, start + 6))

        def both(ref, first, k, low, high):
            return merged(rows_of(ref, *first, k), rows_of(ref, *first, K), k, low, high)

        def leave(first, solved):
            for k in range(K):
                for part, x in zip(strided, solved[k].parts, strict=True):
                    pending.append((res, (first + k, part), x))

        mix = [Batch(dext[k, part] for part in strided) for k in range(K - 1)]
        gu = [both(cx, (0,), k, 0, B - 1) for k in range(K)]
        un = [both(new, (0,), k, 1, B - 1) for k in range(K)]
        (un,) = solve([un], [mix[k] * (gu[k] * gu[k + 1]) for k in range(K - 1)])
        leave(0, un)
        gv = [rows_of(cy, 0, k) for k in range(K)]
        vn = [both(new, (1,), k, 1, B - 1) for k in range(K)]
        (vn,) = solve([vn], [mix[k] * (gv[k] * gv[k + 1]) for k in range(K - 1)])
        leave(K, vn)
        w = [rows_of(wet, k) for k in range(K)]
        mix = [mix[k] * (w[k] * w[k + 1]) for k in range(K - 1)]
        x = [[both(tr, (t,), k, 2, B - 2) for k in range(K)] for t in range(T)]
        for t, solved in enumerate(solve(x, mix)):
            leave(2 * K + t * K, solved)
        flush(pending)


def stepped(nlat, nlon, u, v, q, m, d):
    hbm = pl.BlockSpec(memory_space=pltpu.HBM)
    return pl.pallas_call(
        functools.partial(step, nlat, nlon),
        out_shape=jax.ShapeDtypeStruct(((2 + T) * K, E, B), F32),
        in_specs=[hbm] * 5,
        out_specs=pl.BlockSpec(memory_space=pltpu.VMEM),
        scratch_shapes=[
            pltpu.VMEM((32, E, B), F32),
            pltpu.VMEM((K, B, B), jnp.int32),
            pltpu.VMEM((K - 1, E, B), F32),
            pltpu.VMEM(((2 + T) * K, H, B), F32),
            pltpu.VMEM(((2 + T) * K, H, B), F32),
            pltpu.VMEM((K, H, B), jnp.int32),
            pltpu.VMEM((K, H, B), jnp.int32),
            pltpu.VMEM((B + 4 * H, B), F32),
            pltpu.VMEM((B + 4 * H, B), F32),
            pltpu.VMEM((E, B), F32),
            pltpu.VMEM((E, B), F32),
            pltpu.VMEM((len(FIELDS), E, B), F32),
            pltpu.VMEM((2, K + 2, R, 8, B), F32),
            pltpu.VMEM((2, K + 1, R, 8, B), F32),
            pltpu.VMEM((T, K + 2, R, 8, B), F32),
            pltpu.VMEM((K + 2, R, 8, B), F32),
            pltpu.VMEM((6, K + 2, R, 8, B), F32),
            pltpu.VMEM((3, K + 2, R, 8, B), F32),
            pltpu.VMEM((2, K + 2, 8, B), F32),
            pltpu.VMEM((2, R, 8, B), F32),
            pltpu.SemaphoreType.DMA((7,)),
            pltpu.SemaphoreType.DMA((14,)),
            pltpu.SemaphoreType.DMA((14,)),
        ],
        compiler_params=pltpu.CompilerParams(
            collective_id=0, has_side_effects=True, vmem_limit_bytes=40 * 2**20
        ),
    )(u, v, q, m, d)


def deliver(res, u, v, q, done):
    middle = pl.ds(H, B)
    copies = [
        pltpu.make_async_copy(res.at[0:K, middle], u, done.at[0]),
        pltpu.make_async_copy(res.at[K : 2 * K, middle], v, done.at[1]),
        pltpu.make_async_copy(res.at[2 * K :, middle], q, done.at[2]),
    ]
    for copy in copies:
        copy.start()
    for copy in copies:
        copy.wait()


def delivered(res):
    return pl.pallas_call(
        deliver,
        out_shape=(
            jax.ShapeDtypeStruct((K, B, B), F32),
            jax.ShapeDtypeStruct((K, B, B), F32),
            jax.ShapeDtypeStruct((T * K, B, B), F32),
        ),
        in_specs=[pl.BlockSpec(memory_space=pltpu.VMEM)],
        out_specs=[pl.BlockSpec(memory_space=pltpu.HBM)] * 3,
        scratch_shapes=[pltpu.SemaphoreType.DMA((3,))],
    )(res)


def per_device(nlat, nlon, zonal_flow, meridional_flow, tracers, sea_mask, diffusivity):
    q = tracers.reshape(T * K, B, B)
    given = [
        pltpu.with_memory_space_constraint(x, pltpu.HBM)
        for x in (zonal_flow, meridional_flow, q, sea_mask, diffusivity)
    ]
    res = pltpu.with_memory_space_constraint(stepped(nlat, nlon, *given), pltpu.VMEM)
    u, v, q = delivered(res)
    return u, v, q.reshape(T, K, B, B)


def solution(mesh):
    cells = P(None, "lat", "lon")
    traced = P(None, None, "lat", "lon")
    return jax.shard_map(
        functools.partial(per_device, mesh.shape["lat"], mesh.shape["lon"]),
        mesh=mesh,
        in_specs=(cells, cells, traced, cells, cells),
        out_specs=(cells, cells, traced),
        check_vma=False,
    )
```

time: 25.3 us -> 23.4 us (0.925)
  the two profiles are of different devices: /device:TPU:30 before, /device:TPU:31 now
where the time goes in v2:
time: 23.4 us; the launch traced here: 23.2 us
  Pallas kernels  22.6 us (97%)
  between operations  0.64 us (3%)
    pallas_call x1, Pallas kernels, stepped(): pl.pallas_call(functools.partial(step, nlat, nlon), out_shape=jax.ShapeDt...  21.5 us
    pallas_call x1, Pallas kernels, delivered(): pl.pallas_call(deliver, out_shape=(jax.ShapeDtypeStruct((K, B, B), F32),...  1.08 us

profile of v2, /device:TPU:31, one launch (start us, length us, event | category | flops | bytes accessed | tf_op | source)
XLA Modules:
  0.0 23.2 jit_solution(5101913414657846622)
XLA Ops:
  0.6 21.5 %shard_map.76.res = f32[20,144,128]{2,1,0:T(8,128)S(1)} custom-call(f32[4,128,128]{2,1,0:T(8,128)} %u.1, f32[4,128,128]{2,1,0:T(8,128)} %v.1, f32[12,128,128]{2,1,0:T(8,128)} %bitcast.2, s32[4,128,128]{2,1,0:T(8,128)} %m.1, f32[3,128,128]{2,1,0:T(8,128)} %d.1), custom_call_target="tpu_custom_call" | custom-call | tf_op jit(solution)/shard_map/pallas_call | solution.py:755
  22.1 1.1 %shard_map.77 = (f32[4,128,128]{2,1,0:T(8,128)}, f32[4,128,128]{2,1,0:T(8,128)}, f32[12,128,128]{2,1,0:T(8,128)}) custom-call(f32[20,144,128]{2,1,0:T(8,128)S(1)} %shard_map.76.res), custom_call_target="tpu_custom_call" | custom-call | tf_op jit(solution)/shard_map/pallas_call | solution.py:805

commit v3 on v2

--- a/solution.py
+++ b/solution.py
@@ -19,6 +19,9 @@
 DEPTH = R
 WET, U, V, Q = 4, 8, 12, 16
 FIELDS = (WET, U, V, Q, Q + K, Q + 2 * K)
+DEPTHS = [(f, 4 if U <= f < V else 5 if V <= f < Q else 6) for f in range(WET, Q + T * K)]
+ROWS = [(f, n, sum(m for _, m in DEPTHS[:i])) for i, (f, n) in enumerate(DEPTHS)]
+SENT = -(-sum(n for _, n in DEPTHS) // 8) * 8
 F32 = jnp.float32
 MESH = pl.DeviceIdType.MESH
 coriolis_peak = 0.5
@@ -133,7 +136,7 @@
 
 def step(
     nlat, nlon, u, v, q, m, d, res,
-    ext, mext, dext, hn, hs, hmn, hms, pe, pw, ke, kw, pn, flow, new, tr, wet, cx, cy, fold, cor, load, send, recv,
+    ext, mext, dext, hn, hs, pe, pw, kn, ks, ke, kw, pn, flow, new, tr, wet, cx, cy, fold, cor, load, send, recv,
 ):
     lat = lax.axis_index("lat")
     lon = lax.axis_index("lon")
@@ -197,22 +200,29 @@
             device_id_type=MESH,
         )
 
-    hi = pl.ds(B - H, H)
     lo = pl.ds(0, H)
     lo_held = pl.ds(H, H)
     hi_held = pl.ds(B, H)
 
-    def rows(part, fields, marks, base, row, column):
-        return [
-            remote(u.at[:, part], fields.at[0:K], base, row, column),
-            remote(v.at[:, part], fields.at[K : 2 * K], base + 1, row, column),
-            remote(q.at[:, part], fields.at[2 * K :], base + 2, row, column),
-            remote(m.at[:, part], marks, base + 3, row, column),
-        ]
-
-    to_north = rows(hi, hs, hms, 8, n_lat, n_mid)
-    over_fold = rows(hi, hn, hmn, 2, n_lat, n_mid)
-    to_south = rows(lo, hn, hmn, 2, s_lat, lon)
+    sent, arrived = pl.ds(0, SENT), pl.ds(H, SENT)
+    to_north = [remote(kn.at[sent], hs.at[arrived], 5, n_lat, n_mid)]
+    over_fold = [remote(kn.at[sent], hn.at[arrived], 2, n_lat, n_mid)]
+    to_south = [remote(ks.at[sent], hn.at[arrived], 2, s_lat, lon)]
+
+    own_rows, lo_pack, hi_pack = pl.ds(H, B), pl.ds(0, 2 * H), pl.ds(B, 2 * H)
+    lo_land, mid_land, hi_land = pl.ds(0, 2 * H), pl.ds(2 * H, B), pl.ds(2 * H + B, 2 * H)
+    sends = [
+        remote(ke.at[own_rows], pw.at[mid_land], 1, lat, east),
+        remote(kw.at[own_rows], pe.at[mid_land], 0, lat, west),
+    ]
+    north_east = remote(ke.at[hi_pack], pw.at[lo_land], 7, n_lat, n_east)
+    north_west = remote(kw.at[hi_pack], pe.at[lo_land], 6, n_lat, n_west)
+    fold_west = remote(kw.at[hi_pack], pw.at[hi_land], 4, n_lat, n_west)
+    fold_east = remote(ke.at[hi_pack], pe.at[hi_land], 3, n_lat, n_east)
+    self_west = pltpu.make_async_copy(kw.at[hi_pack], pw.at[hi_land], load.at[5])
+    self_east = pltpu.make_async_copy(ke.at[hi_pack], pe.at[hi_land], load.at[6])
+    south_east = remote(ke.at[lo_pack], pw.at[hi_land], 4, s_lat, east)
+    south_west = remote(kw.at[lo_pack], pe.at[hi_land], 3, s_lat, west)
 
     def enter():
         peers = (
@@ -223,6 +233,32 @@
         )
         pl.semaphore_wait(barrier, peers)
 
+        @pl.when(jnp.logical_not(top))
+        def _():
+            north_east.start()
+            north_west.start()
+
+        @pl.when(top & own_w)
+        def _():
+            self_west.start()
+
+        @pl.when(top & jnp.logical_not(own_w))
+        def _():
+            fold_west.start()
+
+        @pl.when(top & own_e)
+        def _():
+            self_east.start()
+
+        @pl.when(top & jnp.logical_not(own_e))
+        def _():
+            fold_east.start()
+
+        @pl.when(jnp.logical_not(bottom))
+        def _():
+            south_east.start()
+            south_west.start()
+
         @pl.when(top)
         def _():
             for copy in over_fold:
@@ -238,33 +274,18 @@
             for copy in to_south:
                 copy.start()
 
-    reached_late = lon >= nlon // 2
-
-    @pl.when(reached_late)
-    def _():
-        enter()
-
     lane = lax.broadcasted_iota(jnp.int32, (8, B), 1)
     sub = lax.broadcasted_iota(jnp.int32, (8, B), 0)
     group = lane // 8
-    own_rows, lo_pack, hi_pack = pl.ds(H, B), pl.ds(0, 2 * H), pl.ds(B, 2 * H)
-    lo_land, mid_land, hi_land = pl.ds(0, 2 * H), pl.ds(2 * H, B), pl.ds(2 * H + B, 2 * H)
-    sends = [
-        remote(ke.at[own_rows], pw.at[mid_land], 1, lat, east),
-        remote(kw.at[own_rows], pe.at[mid_land], 0, lat, west),
-    ]
-    north_east = remote(ke.at[hi_pack], pw.at[lo_land], 13, n_lat, n_east)
-    north_west = remote(kw.at[hi_pack], pe.at[lo_land], 12, n_lat, n_west)
-    fold_west = remote(kw.at[hi_pack], pw.at[hi_land], 7, n_lat, n_west)
-    fold_east = remote(ke.at[hi_pack], pe.at[hi_land], 6, n_lat, n_east)
-    self_west = pltpu.make_async_copy(kw.at[hi_pack], pw.at[hi_land], load.at[5])
-    self_east = pltpu.make_async_copy(ke.at[hi_pack], pe.at[hi_land], load.at[6])
-    south_east = remote(ke.at[lo_pack], pw.at[hi_land], 7, s_lat, east)
-    south_west = remote(kw.at[lo_pack], pe.at[hi_land], 6, s_lat, west)
+
+    reached_late = lon >= nlon // 2
 
     for f in range(WET, Q + T * K):
         ext[f, lo] = jnp.zeros((H, B), F32)
         ext[f, beyond] = jnp.zeros((H, B), F32)
+    for landing in (hn, hs):
+        landing[lo] = jnp.zeros((H, B), F32)
+        landing[pl.ds(H + SENT, H)] = jnp.zeros((H, B), F32)
     for copy in loads:
         copy.wait()
 
@@ -279,78 +300,67 @@
     )
     spare_of = jnp.minimum(spare_of, B - 1)
 
-    blocks = [pl.ds(i * 8, 8) for i in range(B // 8)]
     held_blocks = [pl.ds(i * 8 + H, 8) for i in range(B // 8)]
-
-    def read(ref, *index):
-        return Batch(ref[(*index, part)] for part in held_blocks)
+    inner_blocks = held_blocks[1:-1]
+    outer_blocks = [lo_held, hi_held]
+
+    def read(ref, *index, parts=held_blocks):
+        return Batch(ref[(*index, part)] for part in parts)
 
     pending = []
 
-    def write(ref, index, x):
-        for part, y in zip(held_blocks, x.parts, strict=True):
+    def write(ref, index, x, parts=held_blocks):
+        for part, y in zip(parts, x.parts, strict=True):
             pending.append((ref, (*index, part), y))
 
-    packed_w = packed_e = Batch([jnp.zeros((8, B), F32)] * len(blocks))
     for k in range(K):
-        sea = Batch(mext[k, part].astype(F32) for part in blocks)
+        sea = Batch(mext[k, pl.ds(i * 8, 8)].astype(F32) for i in range(B // 8))
         write(ext, (WET + k,), sea)
-        for f in range(T + 1):
-            j = 4 * k + f
-            x = rolled(read(ext, Q + f * K + k) if f < T else sea, 8 * j)
-            packed_w = where(group == j, x, packed_w)
-            packed_e = where(group == (j - 1) % 16, x, packed_e)
-        x = picked(read(ext, V + k), spare_of)
-        packed_w = where(spare_w & (level == k), x, packed_w)
-        packed_e = where(spare_e & (level == k), x, packed_e)
-    write(kw, (), packed_w)
-    write(ke, (), packed_e)
     flush(pending)
-    for first, held in ((0, lo_held), (B + H, hi_held)):
-        packed_w = jnp.zeros((8, B), F32)
-        packed_e = jnp.zeros((8, B), F32)
+
+    def pack(parts):
+        packed_w = packed_e = Batch([jnp.zeros((8, B), F32)] * len(parts))
+        for k in range(K):
+            for f, field in enumerate((Q, Q + K, Q + 2 * K, WET)):
+                j = 4 * k + f
+                x = rolled(read(ext, field + k, parts=parts), 8 * j)
+                packed_w = where(group == j, x, packed_w)
+                packed_e = where(group == (j - 1) % 16, x, packed_e)
+            x = picked(read(ext, V + k, parts=parts), spare_of)
+            packed_w = where(spare_w & (level == k), x, packed_w)
+            packed_e = where(spare_e & (level == k), x, packed_e)
+        write(kw, (), packed_w, parts)
+        write(ke, (), packed_e, parts)
+
+    def pack_flow(parts, into):
+        packed_w = packed_e = Batch([jnp.zeros((8, B), F32)] * len(parts))
         for k in range(K):
             for f, field in enumerate((U, V)):
                 j = 4 * k + f
-                x = rolled(ext[field + k, held], 8 * j)
-                packed_w = jnp.where(group == j, x, packed_w)
-                packed_e = jnp.where(group == (j - 1) % 16, x, packed_e)
-        kw[pl.ds(first, 8)] = packed_w
-        ke[pl.ds(first, 8)] = packed_e
-
-    def enter_columns():
-        @pl.when(jnp.logical_not(top))
-        def _():
-            north_east.start()
-            north_west.start()
-
-        @pl.when(top & own_w)
-        def _():
-            self_west.start()
-
-        @pl.when(top & jnp.logical_not(own_w))
-        def _():
-            fold_west.start()
-
-        @pl.when(top & own_e)
-        def _():
-            self_east.start()
-
-        @pl.when(top & jnp.logical_not(own_e))
-        def _():
-            fold_east.start()
-
-        @pl.when(jnp.logical_not(bottom))
-        def _():
-            south_east.start()
-            south_west.start()
-
+                x = rolled(read(ext, field + k, parts=parts), 8 * j)
+                packed_w = where(group == j, x, packed_w)
+                packed_e = where(group == (j - 1) % 16, x, packed_e)
+        write(kw, (), packed_w, into)
+        write(ke, (), packed_e, into)
+
+    pack(outer_blocks)
+    pack_flow(outer_blocks, [lo, beyond])
+    flush(pending)
+    for f, n, at in ROWS:
+        kn[pl.ds(at, 8)] = ext[f, pl.ds(H + B - n, 8)]
+        ks[pl.ds(at, 8)] = ext[f, lo_held]
+
+    @pl.when(reached_late)
+    def _():
+        enter()
+
+    pack(inner_blocks)
+    flush(pending)
+
+    @pl.when(reached_late)
+    def _():
         for copy in sends:
             copy.start()
-
-    @pl.when(reached_late)
-    def _():
-        enter_columns()
 
     far_hi = (place >= 10) & (place < 16)
     far_lo = (place >= 16) & (place < 22)
@@ -383,7 +393,8 @@
     @pl.when(jnp.logical_not(reached_late))
     def _():
         enter()
-        enter_columns()
+        for copy in sends:
+            copy.start()
 
     def coriolis(offset):
         row = lat * B + R * sub + lane - H
@@ -610,13 +621,9 @@
         north_west.wait_recv()
 
 
-    for n, field in enumerate((U, V, Q, Q + K, Q + 2 * K)):
-        for k in range(K):
-            pending.append((ext, (field + k, lo), hs[n * K + k]))
-            pending.append((ext, (field + k, beyond), hn[n * K + k]))
-    for k in range(K):
-        pending.append((ext, (WET + k, lo), hms[k].astype(F32)))
-        pending.append((ext, (WET + k, beyond), hmn[k].astype(F32)))
+    for f, n, at in ROWS:
+        pending.append((ext, (f, lo), hs[pl.ds(at + n, 8)]))
+        pending.append((ext, (f, beyond), hn[pl.ds(at + H, 8)]))
     flush(pending)
 
     @pl.when(bottom)
@@ -629,7 +636,7 @@
     @pl.when(top)
     def _():
         whole = B - 1 - lane
-        turned = [flipped(ext[f, beyond], whole) for f in range(WET, Q + T * K)]
+        turned = [flipped(hn[pl.ds(at + n, 8)], whole) for _, n, at in ROWS]
         for f, x in enumerate(turned, WET):
             ext[f, beyond] = -x if U <= f < Q else x
         within = 7 - lane % 8
@@ -761,12 +768,12 @@
             pltpu.VMEM((32, E, B), F32),
             pltpu.VMEM((K, B, B), jnp.int32),
             pltpu.VMEM((K - 1, E, B), F32),
-            pltpu.VMEM(((2 + T) * K, H, B), F32),
-            pltpu.VMEM(((2 + T) * K, H, B), F32),
-            pltpu.VMEM((K, H, B), jnp.int32),
-            pltpu.VMEM((K, H, B), jnp.int32),
+            pltpu.VMEM((SENT + 2 * H, B), F32),
+            pltpu.VMEM((SENT + 2 * H, B), F32),
             pltpu.VMEM((B + 4 * H, B), F32),
             pltpu.VMEM((B + 4 * H, B), F32),
+            pltpu.VMEM((SENT + H, B), F32),
+            pltpu.VMEM((SENT + H, B), F32),
             pltpu.VMEM((E, B), F32),
             pltpu.VMEM((E, B), F32),
             pltpu.VMEM((len(FIELDS), E, B), F32),
@@ -779,8 +786,8 @@
             pltpu.VMEM((2, K + 2, 8, B), F32),
             pltpu.VMEM((2, R, 8, B), F32),
             pltpu.SemaphoreType.DMA((7,)),
-            pltpu.SemaphoreType.DMA((14,)),
-            pltpu.SemaphoreType.DMA((14,)),
+            pltpu.SemaphoreType.DMA((8,)),
+            pltpu.SemaphoreType.DMA((8,)),
         ],
         compiler_params=pltpu.CompilerParams(
             collective_id=0, has_side_effects=True, vmem_limit_bytes=40 * 2**20

time: 23.4 us -> 22 us (0.940)
  Pallas kernels: 22.6 us -> 21.3 us
    pallas_call x1, Pallas kernels: 21.5 us -> 20.2 us  [stepped(): pl.pallas_call(functools.partial(step, nlat, nlon), out_shape=jax.ShapeDt...]
where the time goes in v3:
time: 22 us; the launch traced here: 21.9 us
  Pallas kernels  21.3 us (97%)
  between operations  0.64 us (3%)
    pallas_call x1, Pallas kernels, stepped(): pl.pallas_call(functools.partial(step, nlat, nlon), out_shape=jax.ShapeDt...  20.2 us
    pallas_call x1, Pallas kernels, delivered(): pl.pallas_call(deliver, out_shape=(jax.ShapeDtypeStruct((K, B, B), F32),...  1.08 us

profile of v3, /device:TPU:31, one launch (start us, length us, event | category | flops | bytes accessed | tf_op | source)
XLA Modules:
  0.0 21.9 jit_solution(6445630082706473743)
XLA Ops:
  0.6 20.2 %shard_map.76.res = f32[20,144,128]{2,1,0:T(8,128)S(1)} custom-call(f32[4,128,128]{2,1,0:T(8,128)} %u.1, f32[4,128,128]{2,1,0:T(8,128)} %v.1, f32[12,128,128]{2,1,0:T(8,128)} %bitcast.2, s32[4,128,128]{2,1,0:T(8,128)} %m.1, f32[3,128,128]{2,1,0:T(8,128)} %d.1), custom_call_target="tpu_custom_call" | custom-call | tf_op jit(solution)/shard_map/pallas_call | solution.py:762
  20.8 1.1 %shard_map.77 = (f32[4,128,128]{2,1,0:T(8,128)}, f32[4,128,128]{2,1,0:T(8,128)}, f32[12,128,128]{2,1,0:T(8,128)}) custom-call(f32[20,144,128]{2,1,0:T(8,128)S(1)} %shard_map.76.res), custom_call_target="tpu_custom_call" | custom-call | tf_op jit(solution)/shard_map/pallas_call | solution.py:812

commit v4 on v3

--- a/solution.py
+++ b/solution.py
@@ -104,13 +104,19 @@
     return each(lambda part: jnp.take_along_axis(part, index, axis=1), x)
 
 
+def merged(x, edge, k, low, high):
+    lane = lax.broadcasted_iota(jnp.int32, (8, B), 1)
+    source = jnp.where(lane < B // 2, lane + 32 * k + 22, lane + 32 * k + 10) % B
+    return where((lane < low) | (lane >= high), picked(edge, source), x)
+
+
 def flipped(x, index):
     x = jnp.take_along_axis(x, index, axis=1)
     backward = 7 - lax.broadcasted_iota(jnp.int32, (8, B), 0)
     return jnp.take_along_axis(x, backward, axis=0)
 
 
-def solve(x, coupling):
+def factored(coupling):
     carried = []
     inverse = []
     for k in range(K):
@@ -122,21 +128,22 @@
         inverse.append(1.0 / divisor)
         if k < K - 1:
             carried.append(coupling[k] * inverse[k])
-    results = []
-    for field in x:
-        scaled = [field[0] * inverse[0]]
-        for k in range(1, K):
-            scaled.append((field[k] + coupling[k - 1] * scaled[k - 1]) * inverse[k])
-        solved = [scaled[K - 1]]
-        for k in range(K - 2, -1, -1):
-            solved.insert(0, scaled[k] + carried[k] * solved[0])
-        results.append(solved)
-    return results
+    return inverse, carried
+
+
+def solve(x, coupling, inverse, carried):
+    scaled = [x[0] * inverse[0]]
+    for k in range(1, K):
+        scaled.append((x[k] + coupling[k - 1] * scaled[k - 1]) * inverse[k])
+    solved = [scaled[K - 1]]
+    for k in range(K - 2, -1, -1):
+        solved.insert(0, scaled[k] + carried[k] * solved[0])
+    return solved
 
 
 def step(
-    nlat, nlon, u, v, q, m, d, res,
-    ext, mext, dext, hn, hs, pe, pw, kn, ks, ke, kw, pn, flow, new, tr, wet, cx, cy, fold, cor, load, send, recv,
+    nlat, nlon, u, v, q, m, d, res, tr, wet, dext,
+    ext, mext, hn, hs, pe, pw, kn, ks, ke, kw, pn, flow, new, cx, cy, fold, cor, load, send, recv,
 ):
     lat = lax.axis_index("lat")
     lon = lax.axis_index("lon")
@@ -157,21 +164,30 @@
 
     middle = pl.ds(H, B)
     beyond = pl.ds(H + B, H)
-    loads = [
-        pltpu.make_async_copy(u, ext.at[U : U + K, middle], load.at[0]),
-        pltpu.make_async_copy(v, ext.at[V : V + K, middle], load.at[1]),
-        pltpu.make_async_copy(q, ext.at[Q : Q + T * K, middle], load.at[2]),
-        pltpu.make_async_copy(m, mext, load.at[3]),
-        pltpu.make_async_copy(d, dext.at[:, middle], load.at[4]),
-    ]
-    for copy in loads:
-        copy.start()
-
     barrier = pltpu.get_barrier_semaphore()
 
     def greet(row, column):
         pl.semaphore_signal(barrier, inc=1, device_id=at(row, column), device_id_type=MESH)
 
+    lo = pl.ds(0, H)
+    lo_held = pl.ds(H, H)
+    hi_held = pl.ds(B, H)
+
+    def fetch(part, held, slot):
+        u_held, v_held, q_held = (ext.at[f : f + n, held] for f, n in ((U, K), (V, K), (Q, T * K)))
+        return [
+            pltpu.make_async_copy(u.at[:, part], u_held, load.at[slot]),
+            pltpu.make_async_copy(v.at[:, part], v_held, load.at[slot + 1]),
+            pltpu.make_async_copy(q.at[:, part], q_held, load.at[slot + 2]),
+            pltpu.make_async_copy(m.at[:, part], mext.at[:, part], load.at[slot + 3]),
+        ]
+
+    outer_loads = fetch(lo, lo_held, 0) + fetch(pl.ds(B - H, H), hi_held, 4)
+    inner_loads = fetch(pl.ds(H, B - 2 * H), pl.ds(2 * H, B - 2 * H), 8)
+    inner_loads.append(pltpu.make_async_copy(d, dext.at[:, middle], load.at[12]))
+
+    for copy in outer_loads:
+        copy.start()
     greet(lat, east)
     greet(lat, west)
     greet(n_lat, n_mid)
@@ -189,6 +205,9 @@
         greet(s_lat, lon)
         greet(s_lat, west)
         greet(s_lat, east)
+
+    for copy in inner_loads:
+        copy.start()
 
     def remote(src, dst, slot, row, column):
         return pltpu.make_async_remote_copy(
@@ -200,9 +219,6 @@
             device_id_type=MESH,
         )
 
-    lo = pl.ds(0, H)
-    lo_held = pl.ds(H, H)
-    hi_held = pl.ds(B, H)
 
     sent, arrived = pl.ds(0, SENT), pl.ds(H, SENT)
     to_north = [remote(kn.at[sent], hs.at[arrived], 5, n_lat, n_mid)]
@@ -219,8 +235,8 @@
     north_west = remote(kw.at[hi_pack], pe.at[lo_land], 6, n_lat, n_west)
     fold_west = remote(kw.at[hi_pack], pw.at[hi_land], 4, n_lat, n_west)
     fold_east = remote(ke.at[hi_pack], pe.at[hi_land], 3, n_lat, n_east)
-    self_west = pltpu.make_async_copy(kw.at[hi_pack], pw.at[hi_land], load.at[5])
-    self_east = pltpu.make_async_copy(ke.at[hi_pack], pe.at[hi_land], load.at[6])
+    self_west = pltpu.make_async_copy(kw.at[hi_pack], pw.at[hi_land], load.at[13])
+    self_east = pltpu.make_async_copy(ke.at[hi_pack], pe.at[hi_land], load.at[14])
     south_east = remote(ke.at[lo_pack], pw.at[hi_land], 4, s_lat, east)
     south_west = remote(kw.at[lo_pack], pe.at[hi_land], 3, s_lat, west)
 
@@ -286,7 +302,7 @@
     for landing in (hn, hs):
         landing[lo] = jnp.zeros((H, B), F32)
         landing[pl.ds(H + SENT, H)] = jnp.zeros((H, B), F32)
-    for copy in loads:
+    for copy in outer_loads:
         copy.wait()
 
     place = lane % 32
@@ -313,10 +329,11 @@
         for part, y in zip(parts, x.parts, strict=True):
             pending.append((ref, (*index, part), y))
 
-    for k in range(K):
-        sea = Batch(mext[k, pl.ds(i * 8, 8)].astype(F32) for i in range(B // 8))
-        write(ext, (WET + k,), sea)
-    flush(pending)
+    def convert(parts):
+        for k in range(K):
+            for part in parts:
+                pending.append((ext, (WET + k, part), mext[k, pl.ds(part.start - H, 8)].astype(F32)))
+        flush(pending)
 
     def pack(parts):
         packed_w = packed_e = Batch([jnp.zeros((8, B), F32)] * len(parts))
@@ -343,6 +360,7 @@
         write(kw, (), packed_w, into)
         write(ke, (), packed_e, into)
 
+    convert(outer_blocks)
     pack(outer_blocks)
     pack_flow(outer_blocks, [lo, beyond])
     flush(pending)
@@ -354,6 +372,9 @@
     def _():
         enter()
 
+    for copy in inner_loads:
+        copy.wait()
+    convert(inner_blocks)
     pack(inner_blocks)
     flush(pending)
 
@@ -406,32 +427,32 @@
         for r in range(R):
             cor[f, r] = jnp.broadcast_to(turning[:, r : r + 1], (8, B))
 
-    def prepare(i, rows, count, bend, beyond_fold, momentum):
-        def get(f, r):
+    def prepare(cells, count, bend, beyond_fold, momentum, size=9):
+        def get(f, i, r):
             if r == -1:
                 return below(flow[f, i, count - 1])
             if r == count:
                 return above(flow[f, i, 0])
             return flow[f, i, r]
 
-        for start in range(0, len(rows), 9):
-            chunk = rows[start : start + 9]
+        for start in range(0, len(cells), size):
+            chunk = cells[start : start + size]
 
             def put(ref, index, x):
-                for r, y in zip(chunk, x.parts, strict=True):
+                for (i, r), y in zip(chunk, x.parts, strict=True):
                     held_back.append((ref, (index, i, r), y))
 
             def bent(a, b):
                 return Batch(
                     jnp.where(beyond_fold, x, y) if r > bend else y
-                    for r, x, y in zip(chunk, a.parts, b.parts, strict=True)
+                    for (_, r), x, y in zip(chunk, a.parts, b.parts, strict=True)
                 )
 
             held_back = []
-            u0, v0 = (Batch(get(f, r) for r in chunk) for f in range(2))
-            un, vn = (Batch(get(f, r + 1) for r in chunk) for f in range(2))
-            w0 = Batch(wet[i, r] for r in chunk)
-            wn = Batch(wet[i, r + 1] if r < count - 1 else above(wet[i, 0]) for r in chunk)
+            u0, v0 = (Batch(get(f, i, r) for i, r in chunk) for f in range(2))
+            un, vn = (Batch(get(f, i, r + 1) for i, r in chunk) for f in range(2))
+            w0 = Batch(wet[i, r] for i, r in chunk)
+            wn = Batch(wet[i, r + 1] if r < count - 1 else above(wet[i, 0]) for i, r in chunk)
             gu = w0 * following(w0)
             gv = w0 * wn
             ue = following(u0)
@@ -449,14 +470,14 @@
             put(cy, 0, gv)
             put(cy, 1, va * gv)
             put(cy, 2, where(va > 0.0, 0.5, -0.5) - 0.5 * va)
-            if bend in chunk:
-                n = chunk.index(bend)
-                vf = jnp.where(beyond_fold, vn.parts[n], v0.parts[n])
-                held_back.append((fold, (0, i), vf * gv.parts[n]))
-                held_back.append((fold, (1, i), jnp.where(vf > 0.0, 0.5, -0.5) - 0.5 * vf))
+            for n, (i, r) in enumerate(chunk):
+                if r == bend:
+                    vf = jnp.where(beyond_fold, vn.parts[n], v0.parts[n])
+                    held_back.append((fold, (0, i), vf * gv.parts[n]))
+                    held_back.append((fold, (1, i), jnp.where(vf > 0.0, 0.5, -0.5) - 0.5 * vf))
             if momentum:
-                us, vs = (Batch(get(f, r - 1) for r in chunk) for f in range(2))
-                turn_u, turn_v = (Batch(cor[f, r] for r in chunk) for f in range(2))
+                us, vs = (Batch(get(f, i, r - 1) for i, r in chunk) for f in range(2))
+                turn_u, turn_v = (Batch(cor[f, r] for _, r in chunk) for f in range(2))
                 a = v0 + vs
                 vbar = 0.25 * (a + following(a))
                 a = u0 + un
@@ -472,7 +493,7 @@
     bend = R - H - 1
 
     def prepare_level(rows, i, carry):
-        prepare(i, rows, R, bend, last, True)
+        prepare([(i, r) for r in rows], R, bend, last, True)
         return carry
 
     lax.fori_loop(0, K, functools.partial(prepare_level, range(R)), 0)
@@ -655,10 +676,22 @@
             pending.append((pn, (n, part), y))
 
     corners = ((lo, beyond), (lo, pl.ds(3 * H + B, H)), (pl.ds(H, H), pl.ds(2 * H + B, H)))
-    for n, slot in ((0, 3), (3, 0), (4, 1), (5, 2), (1, 0), (2, 1)):
-        landed = corners[2] if n in (1, 2) else corners[1]
-        pack_e, pack_w = (Batch(pack[part] for part in landed) for pack in (pe, pw))
-        spread(n, corners[0], pack_e, pack_w, slot, edges(FIELDS[n], corners[0]))
+    order = ((0, 3), (3, 0), (4, 1), (5, 2), (1, 0), (2, 1))
+    landings = [corners[2] if n in (1, 2) else corners[1] for n, _ in order]
+    far = [
+        [rolled(Batch(pack[part] for part in landed), offset - 8 * slot) for landed, (_, slot) in zip(landings, order)]
+        for pack, offset in ((pe, 10), (pw, 22))
+    ]
+    picks = [
+        [picked(Batch(ext[FIELDS[n] + k, part] for part in corners[0]), source_of) for k in range(K)] for n, _ in order
+    ]
+    for (n, _), x, far_e, far_w in zip(order, picks, *far):
+        edge = x[0]
+        for k in range(1, K):
+            edge = where(level == k, x[k], edge)
+        edge = where(far_lo, far_w, where(far_hi, far_e, edge))
+        for part, y in zip(corners[0], edge.parts, strict=True):
+            pending.append((pn, (n, part), y))
     landed = [pl.ds(i * 8 + 2 * H, 8) for i in range(B // 8)]
     pack_e, pack_w = (Batch(pack[part] for part in landed) for pack in (pe, pw))
     for n, slot in ((0, 3), (3, 0), (4, 1), (5, 2)):
@@ -697,9 +730,9 @@
         for n in range(3):
             levels(n, r)
         flush(pending)
-    prepare(K, range(R), R, bend, last, True)
-    prepare(K + 1, range(S), S, 7, last_strip, False)
-    lax.fori_loop(0, K, functools.partial(prepare_level, range(6, 11)), 0)
+    prepare([(K, r) for r in range(R)], R, bend, last, True, R)
+    prepare([(K + 1, r) for r in range(S)], S, 7, last_strip, False, S)
+    prepare([(k, r) for k in range(K) for r in range(6, 11)], R, bend, last, True, 20)
 
     def advect_edges(i, carry):
         advect(K, R, bend)
@@ -708,21 +741,23 @@
 
     lax.fori_loop(0, 2, advect_edges, 0)
 
-    def merged(x, edge, k, low, high):
-        source = jnp.where(lane < B // 2, lane + 32 * k + 22, lane + 32 * k + 10) % B
-        return where((lane < low) | (lane >= high), picked(edge, source), x)
-
     ends = (sub == 0) | (sub == 7)
     for t in range(T):
+        strip = [
+            jnp.take_along_axis(tr[t, K + 1, r - 2], jnp.where(sub == 0, k, 4 + k), axis=0)
+            for k in range(K)
+            for r in range(6, 12)
+        ]
+        edge = Batch(tr[t, K, r] for r in range(R))
+        x = [
+            [jnp.where(ends, strip[6 * k + r - 6], tr[t, k, r]) if 6 <= r < 12 else tr[t, k, r] for r in range(R)]
+            for k in range(K)
+        ]
+        x = [merged(Batch(x[k]), edge, k, 4, B - 4) for k in range(K)]
         for k in range(K):
-            source = jnp.where(sub == 0, k, 4 + k)
-            x = [tr[t, k, r] for r in range(R)]
-            for r in range(6, 12):
-                x[r] = jnp.where(ends, jnp.take_along_axis(tr[t, K + 1, r - 2], source, axis=0), x[r])
-            x = merged(Batch(x), Batch(tr[t, K, r] for r in range(R)), k, 4, B - 4)
             for r in range(R):
-                pending.append((tr, (t, k, r), x.parts[r]))
-            flush(pending)
+                pending.append((tr, (t, k, r), x[k].parts[r]))
+        flush(pending)
 
     lax.fori_loop(0, K + 1, advect_level, 0)
 
@@ -743,17 +778,14 @@
         mix = [Batch(dext[k, part] for part in strided) for k in range(K - 1)]
         gu = [both(cx, (0,), k, 0, B - 1) for k in range(K)]
         un = [both(new, (0,), k, 1, B - 1) for k in range(K)]
-        (un,) = solve([un], [mix[k] * (gu[k] * gu[k + 1]) for k in range(K - 1)])
+        coupling = [mix[k] * (gu[k] * gu[k + 1]) for k in range(K - 1)]
+        un = solve(un, coupling, *factored(coupling))
         leave(0, un)
         gv = [rows_of(cy, 0, k) for k in range(K)]
         vn = [both(new, (1,), k, 1, B - 1) for k in range(K)]
-        (vn,) = solve([vn], [mix[k] * (gv[k] * gv[k + 1]) for k in range(K - 1)])
+        coupling = [mix[k] * (gv[k] * gv[k + 1]) for k in range(K - 1)]
+        vn = solve(vn, coupling, *factored(coupling))
         leave(K, vn)
-        w = [rows_of(wet, k) for k in range(K)]
-        mix = [mix[k] * (w[k] * w[k + 1]) for k in range(K - 1)]
-        x = [[both(tr, (t,), k, 2, B - 2) for k in range(K)] for t in range(T)]
-        for t, solved in enumerate(solve(x, mix)):
-            leave(2 * K + t * K, solved)
         flush(pending)
 
 
@@ -761,13 +793,17 @@
     hbm = pl.BlockSpec(memory_space=pltpu.HBM)
     return pl.pallas_call(
         functools.partial(step, nlat, nlon),
-        out_shape=jax.ShapeDtypeStruct(((2 + T) * K, E, B), F32),
+        out_shape=[
+            jax.ShapeDtypeStruct((2 * K, E, B), F32),
+            jax.ShapeDtypeStruct((T, K + 2, R, 8, B), F32),
+            jax.ShapeDtypeStruct((K + 2, R, 8, B), F32),
+            jax.ShapeDtypeStruct((K - 1, E, B), F32),
+        ],
         in_specs=[hbm] * 5,
-        out_specs=pl.BlockSpec(memory_space=pltpu.VMEM),
+        out_specs=[pl.BlockSpec(memory_space=pltpu.VMEM)] * 4,
         scratch_shapes=[
             pltpu.VMEM((32, E, B), F32),
             pltpu.VMEM((K, B, B), jnp.int32),
-            pltpu.VMEM((K - 1, E, B), F32),
             pltpu.VMEM((SENT + 2 * H, B), F32),
             pltpu.VMEM((SENT + 2 * H, B), F32),
             pltpu.VMEM((B + 4 * H, B), F32),
@@ -779,13 +815,11 @@
             pltpu.VMEM((len(FIELDS), E, B), F32),
             pltpu.VMEM((2, K + 2, R, 8, B), F32),
             pltpu.VMEM((2, K + 1, R, 8, B), F32),
-            pltpu.VMEM((T, K + 2, R, 8, B), F32),
-            pltpu.VMEM((K + 2, R, 8, B), F32),
             pltpu.VMEM((6, K + 2, R, 8, B), F32),
             pltpu.VMEM((3, K + 2, R, 8, B), F32),
             pltpu.VMEM((2, K + 2, 8, B), F32),
             pltpu.VMEM((2, R, 8, B), F32),
-            pltpu.SemaphoreType.DMA((7,)),
+            pltpu.SemaphoreType.DMA((15,)),
             pltpu.SemaphoreType.DMA((8,)),
             pltpu.SemaphoreType.DMA((8,)),
         ],
@@ -795,20 +829,36 @@
     )(u, v, q, m, d)
 
 
-def deliver(res, u, v, q, done):
+def deliver(res, tr, wet, dext, u, v, q, out, done):
     middle = pl.ds(H, B)
     copies = [
         pltpu.make_async_copy(res.at[0:K, middle], u, done.at[0]),
         pltpu.make_async_copy(res.at[K : 2 * K, middle], v, done.at[1]),
-        pltpu.make_async_copy(res.at[2 * K :, middle], q, done.at[2]),
     ]
     for copy in copies:
         copy.start()
+    factors = []
+    for start in range(0, R, 6):
+        rows = range(start, start + 6)
+        w = [Batch(wet[k, r] for r in rows) for k in range(K)]
+        mix = [Batch(dext[k, pl.ds(r, 8, stride=R)] for r in rows) for k in range(K - 1)]
+        coupling = [mix[k] * (w[k] * w[k + 1]) for k in range(K - 1)]
+        factors.append((rows, coupling, *factored(coupling)))
+    for t in range(T):
+        for rows, *factor in factors:
+            edge = Batch(tr[t, K, r] for r in rows)
+            x = [merged(Batch(tr[t, k, r] for r in rows), edge, k, 2, B - 2) for k in range(K)]
+            for k, solved in enumerate(solve(x, *factor)):
+                for r, y in zip(rows, solved.parts, strict=True):
+                    out[t * K + k, pl.ds(r, 8, stride=R)] = y
+        part = pl.ds(t * K, K)
+        copies.append(pltpu.make_async_copy(out.at[part, middle], q.at[part], done.at[2 + t]))
+        copies[-1].start()
     for copy in copies:
         copy.wait()
 
 
-def delivered(res):
+def delivered(given):
     return pl.pallas_call(
         deliver,
         out_shape=(
@@ -816,10 +866,10 @@
             jax.ShapeDtypeStruct((K, B, B), F32),
             jax.ShapeDtypeStruct((T * K, B, B), F32),
         ),
-        in_specs=[pl.BlockSpec(memory_space=pltpu.VMEM)],
+        in_specs=[pl.BlockSpec(memory_space=pltpu.VMEM)] * 4,
         out_specs=[pl.BlockSpec(memory_space=pltpu.HBM)] * 3,
-        scratch_shapes=[pltpu.SemaphoreType.DMA((3,))],
-    )(res)
+        scratch_shapes=[pltpu.VMEM((T * K, E, B), F32), pltpu.SemaphoreType.DMA((2 + T,))],
+    )(*given)
 
 
 def per_device(nlat, nlon, zonal_flow, meridional_flow, tracers, sea_mask, diffusivity):
@@ -828,8 +878,8 @@
         pltpu.with_memory_space_constraint(x, pltpu.HBM)
         for x in (zonal_flow, meridional_flow, q, sea_mask, diffusivity)
     ]
-    res = pltpu.with_memory_space_constraint(stepped(nlat, nlon, *given), pltpu.VMEM)
-    u, v, q = delivered(res)
+    kept = [pltpu.with_memory_space_constraint(x, pltpu.VMEM) for x in stepped(nlat, nlon, *given)]
+    u, v, q = delivered(kept)
     return u, v, q.reshape(T, K, B, B)
 
 

time: 22 us -> 21.5 us (0.977)
  Pallas kernels: 21.3 us -> 20.7 us
    pallas_call x1, Pallas kernels: 20.2 us -> 19.6 us  [stepped(): pl.pallas_call(functools.partial(step, nlat, nlon), out_shape=[jax.ShapeD...]
where the time goes in v4:
time: 21.5 us; the launch traced here: 21.4 us
  Pallas kernels  20.7 us (96%)
  between operations  0.64 us (3%)
    pallas_call x1, Pallas kernels, stepped(): pl.pallas_call(functools.partial(step, nlat, nlon), out_shape=[jax.ShapeD...  19.6 us
    pallas_call x1, Pallas kernels, delivered(): pl.pallas_call(deliver, out_shape=(jax.ShapeDtypeStruct((K, B, B), F32),...  1.18 us

profile of v4, /device:TPU:31, one launch (start us, length us, event | category | flops | bytes accessed | tf_op | source)
XLA Modules:
  0.0 21.4 jit_solution(4768347280594265184)
XLA Ops:
  0.6 19.6 %shard_map.76 = (f32[8,144,128]{2,1,0:T(8,128)S(1)}, f32[3,6,18,8,128]{4,3,2,1,0:T(8,128)S(1)}, f32[6,18,8,128]{3,2,1,0:T(8,128)S(1)}, f32[3,144,128]{2,1,0:T(8,128)S(1)}) custom-call(f32[4,128,128]{2,1,0:T(8,128)} %u.1, f32[4,128,128]{2,1,0:T(8,128)} %v.1, f32[12,128,128]{2,1,0:T(8,128)} %bitcast.2, s32[4,128,128]{2,1,0:T(8,128)} %m.1, f32[3,128,128]{2,1,0:T(8,128)} %d.1), custom_call_target="tpu_custom_call" | custom-call | tf_op jit(solution)/shard_map/pallas_call | solution.py:794
  20.2 1.2 %shard_map.77 = (f32[4,128,128]{2,1,0:T(8,128)}, f32[4,128,128]{2,1,0:T(8,128)}, f32[12,128,128]{2,1,0:T(8,128)}) custom-call(f32[8,144,128]{2,1,0:T(8,128)S(1)} %get-tuple-element.10.res, f32[3,6,18,8,128]{4,3,2,1,0:T(8,128)S(1)} %get-tuple-element.11.tr, f32[6,18,8,128]{3,2,1,0:T(8,128)S(1)} %get-tuple-element.12.wet, ...), custom_call_target="tpu_custom_call" | custom-call | tf_op jit(solution)/shard_map/pallas_call | solution.py:862

commit v5 on v4

--- a/solution.py
+++ b/solution.py
@@ -739,7 +739,7 @@
         advect(K + 1, S, 7)
         return carry
 
-    lax.fori_loop(0, 2, advect_edges, 0)
+    lax.fori_loop(0, 2, advect_edges, 0, unroll=True)
 
     ends = (sub == 0) | (sub == 7)
     for t in range(T):
@@ -759,7 +759,7 @@
                 pending.append((tr, (t, k, r), x[k].parts[r]))
         flush(pending)
 
-    lax.fori_loop(0, K + 1, advect_level, 0)
+    lax.fori_loop(0, K + 1, advect_level, 0, unroll=True)
 
     for start in range(0, R, 6):
         strided = [pl.ds(r, 8, stride=R) for r in range(start, start + 6)]

time: 21.5 us -> 20.8 us (0.967)
  Pallas kernels: 20.7 us -> 20.1 us
    pallas_call x1, Pallas kernels: 19.6 us -> 18.9 us  [stepped(): pl.pallas_call(functools.partial(step, nlat, nlon), out_shape=[jax.ShapeD...]
where the time goes in v5:
time: 20.8 us; the launch traced here: 20.7 us
  Pallas kernels  20.1 us (97%)
  between operations  0.64 us (3%)
    pallas_call x1, Pallas kernels, stepped(): pl.pallas_call(functools.partial(step, nlat, nlon), out_shape=[jax.ShapeD...  18.9 us
    pallas_call x1, Pallas kernels, delivered(): pl.pallas_call(deliver, out_shape=(jax.ShapeDtypeStruct((K, B, B), F32),...  1.18 us

profile of v5, /device:TPU:31, one launch (start us, length us, event | category | flops | bytes accessed | tf_op | source)
XLA Modules:
  0.0 20.7 jit_solution(14440688280263846342)
XLA Ops:
  0.6 18.9 %shard_map.76 = (f32[8,144,128]{2,1,0:T(8,128)S(1)}, f32[3,6,18,8,128]{4,3,2,1,0:T(8,128)S(1)}, f32[6,18,8,128]{3,2,1,0:T(8,128)S(1)}, f32[3,144,128]{2,1,0:T(8,128)S(1)}) custom-call(f32[4,128,128]{2,1,0:T(8,128)} %u.1, f32[4,128,128]{2,1,0:T(8,128)} %v.1, f32[12,128,128]{2,1,0:T(8,128)} %bitcast.2, s32[4,128,128]{2,1,0:T(8,128)} %m.1, f32[3,128,128]{2,1,0:T(8,128)} %d.1), custom_call_target="tpu_custom_call" | custom-call | tf_op jit(solution)/shard_map/pallas_call | solution.py:794
  19.5 1.2 %shard_map.77 = (f32[4,128,128]{2,1,0:T(8,128)}, f32[4,128,128]{2,1,0:T(8,128)}, f32[12,128,128]{2,1,0:T(8,128)}) custom-call(f32[8,144,128]{2,1,0:T(8,128)S(1)} %get-tuple-element.10.res, f32[3,6,18,8,128]{4,3,2,1,0:T(8,128)S(1)} %get-tuple-element.11.tr, f32[6,18,8,128]{3,2,1,0:T(8,128)S(1)} %get-tuple-element.12.wet, ...), custom_call_target="tpu_custom_call" | custom-call | tf_op jit(solution)/shard_map/pallas_call | solution.py:862
